TPU v7x, 256 devices: a whole 4x4x8 slice. The times are simulated.
256 devices in a mesh: tok: 8 (over z_lo, y), row: 32 (over x, z_hi, core).
Axes of the slice: x: 4, y: 4, z: 8 (z_hi: 4, z_lo: 2; z = z_hi * 2 + z_lo), core: 2. Of those that a mesh axis runs over, the one named last changes fastest.
Arguments:
- token_ids: int32 [4096], P('tok'), may hold values from 1 to 50271, as said below
- calib_input: bfloat16 [4096, 49152], P('tok', 'row'), may hold values from -6 to 6
- keep_mask: int32 [12288, 256], P('row'), may hold values from 0 to 1, as said below
- weight_window: float32 [12288, 256], P('row'), may hold values from -0.12 to 0.12
- weight_rest: bfloat16 [12288, 48896], P('row', 'tok'), may hold values from -1.5 to 1.5
- factor_window: float32 [256, 256], replicated, as said below
- factor_rest: float32 [256, 48896], P('row', 'tok'), may hold values from -0.72 to 0.72
Outputs:
- pruned_window: float32 [12288, 256], P('row')
- updated_rest: bfloat16 [12288, 48896], P('row', 'tok')
- hessian_rows: float32 [256, 49152], P('tok', 'row')
- window_outputs: bfloat16 [4096, 12288], P(('tok', 'row'))
Inputs may be any that keep to these rules, and one draw needn't show every extreme that they name: `token_ids`: tokens form sequences of 128 positions; in each, live ids of 2 or more come first, then at least one padding id 1. `keep_mask`: in every row, each aligned group of 4 consecutive columns holds exactly two ones. `factor_window`: zero below the diagonal; diagonal entries positive.
All inputs are finite; a program needn't handle non-finite values.
Results may differ from a plain program's by a relative error of at most 0.011.
Values may be sent and summed in bfloat16 or wider, within the bound.
A program may use at most 64 MiB of HBM per device.

v0:
```python
import jax
import jax.numpy as jnp
from jax import lax
from jax.sharding import PartitionSpec as P

BLOCK = 128
NBLK = 2


def from_root(block, axis, holder):
    block = jnp.where(lax.axis_index(axis) == holder, block, jnp.zeros_like(block))
    return lax.psum(block, axis)


def prune_block(weights, keep_float, factor_block):

    def advance(column, state_pair):
        current, errors = state_pair
        values = lax.dynamic_slice_in_dim(current, column, 1, 1)
        kept = lax.dynamic_slice_in_dim(keep_float, column, 1, 1)
        factor_row = lax.dynamic_slice_in_dim(factor_block, column, 1, 0)
        pivot = lax.dynamic_slice_in_dim(factor_row, column, 1, 1)
        error_col = values * (1.0 - kept) / pivot
        current = current - error_col * factor_row
        errors = lax.dynamic_update_slice_in_dim(errors, error_col, column, 1)
        return (current, errors)

    start_errors = jnp.zeros(weights.shape, jnp.float32)
    return lax.fori_loop(0, weights.shape[1], advance, (weights, start_errors))


def prune_window(weights, keep_float, factor_window):
    pruned_blocks = []
    error_blocks = []
    for block_index in range(NBLK):
        low_col = block_index * BLOCK
        high_col = low_col + BLOCK
        pruned_block, error_block = prune_block(
            weights[:, low_col:high_col],
            keep_float[:, low_col:high_col],
            factor_window[low_col:high_col, low_col:high_col],
        )
        if high_col < weights.shape[1]:
            later = weights[:, high_col:] - jnp.dot(
                error_block,
                factor_window[low_col:high_col, high_col:],
                precision=lax.Precision.HIGHEST,
                preferred_element_type=jnp.float32,
            )
            weights = jnp.concatenate([weights[:, :high_col], later], axis=1)
        pruned_blocks.append(pruned_block)
        error_blocks.append(error_block)
    return (jnp.concatenate(pruned_blocks, axis=1), jnp.concatenate(error_blocks, axis=1))


def on_device(
    token_ids, calib_input, keep_mask, weight_window, weight_rest, factor_window, factor_rest
):
    window = weight_window.shape[1]
    live_mask = (token_ids != 1).astype(jnp.bfloat16)
    local_inputs = calib_input[:, :window]
    window_inputs = from_root(local_inputs, "row", 0) * live_mask[:, None]
    total_tokens = token_ids.shape[0] * lax.axis_size("tok")
    summed = lax.psum_scatter(
        lax.dot_general(
            window_inputs, calib_input, (((0,), (0,)), ((), ())), preferred_element_type=jnp.float32
        ),
        "tok",
        scatter_dimension=0,
        tiled=True,
    )
    hessian_rows = summed * (2.0 / total_tokens)
    keep_float = keep_mask.astype(jnp.float32)
    pruned_window, errors = prune_window(weight_window, keep_float, factor_window)
    rest_change = jnp.dot(
        errors,
        lax.all_gather(factor_rest.astype(jnp.bfloat16), "row", axis=0, tiled=True).astype(
            jnp.float32
        ),
        precision=lax.Precision.HIGHEST,
        preferred_element_type=jnp.float32,
    )
    updated_rest = (weight_rest.astype(jnp.float32) - rest_change).astype(jnp.bfloat16)
    pruned_half = pruned_window.astype(jnp.bfloat16)
    local_outputs = lax.dot_general(
        window_inputs, pruned_half, (((1,), (1,)), ((), ())), preferred_element_type=jnp.float32
    ).astype(jnp.bfloat16)
    window_outputs = lax.all_to_all(local_outputs, "row", split_axis=0, concat_axis=1, tiled=True)
    return (pruned_window, updated_rest, hessian_rows, window_outputs)


def solution(mesh):
    return jax.shard_map(
        on_device,
        mesh=mesh,
        in_specs=(
            P("tok"),
            P("tok", "row"),
            P("row", None),
            P("row", None),
            P("row", "tok"),
            P(),
            P("row", "tok"),
        ),
        out_specs=(P("row", None), P("row", "tok"), P("tok", "row"), P(("tok", "row"), None)),
        check_vma=False,
    )
```

profile of v0, /device:TPU:1, one launch (start us, length us, event | category | flops | bytes accessed | tf_op | source)
XLA Modules:
  0.0 720.6 jit_solution(16610695773798790509)
XLA Ops:
  7.2 1.7 slice_select_fusion
  9.0 0.8 compare_convert_fusion
  9.8 286.7 %all-reduce.2.cloned.1.call-done = bf16[512,256]{1,0:T(8,128)(2,1)} async-done(((bf16[512,256]{1,0:T(8,128)(2,1)}), bf16[512,256]{1,0:T(8,128)(2,1)}) %all-reduce.2.cloned.1.call-update) | async-done | bytes 262160 | tf_op jit(solution)/shard_map/psum | solution.py:12
  296.5 3.3 fusion.6
  301.0 187.7 %while.36 = (s32[]{:T(128)}, f32[384,128]{0,1:T(8,128)S(1)}, f32[384,128]{0,1:T(8,128)S(1)}, f32[384,128]{0,1:T(8,128)S(1)}, f32[128,128]{1,0:T(8,128)S(1)}, /*index=5*/s32[]{:T(128)}, s32[]{:T(128)}, s32[]{:T(128)}) while((s32[]{:T(128)}, f32[384,128]{0,1:T(8,128)S(1)}, f32[384,128]{0,1:T(8,128)S(1)}, f32[384,128]{0,1:T(8,128)S(1)}, ...), condition=%wide.region_1.2_spmd, body=%wide.region_0.1_spmd.sunk | while | flops 99459 | bytes 405641 | solution.py:29
  301.7 0.7 fusion.25
  304.6 0.7 fusion.25
  306.1 0.7 fusion.25
  310.5 0.7 fusion.25
  314.9 0.7 fusion.25
  316.3 0.7 fusion.25
  317.8 0.7 fusion.25
  319.3 0.7 fusion.25
  322.2 0.7 fusion.25
  323.7 0.7 fusion.25
  325.1 0.7 fusion.25
  326.6 0.7 fusion.25
  328.1 0.7 fusion.25
  329.5 0.7 fusion.25
  331.0 0.7 fusion.25
  333.9 0.7 fusion.25
  335.4 0.7 fusion.25
  355.9 0.7 fusion.25
  363.3 0.7 fusion.25
  386.7 0.7 fusion.25
  395.5 0.7 fusion.25
  398.4 0.7 fusion.25
  489.4 187.7 %while.37 = (s32[]{:T(128)}, f32[384,128]{0,1:T(8,128)S(1)}, f32[384,128]{0,1:T(8,128)S(1)}, f32[384,128]{0,1:T(8,128)S(1)}, f32[128,128]{1,0:T(8,128)S(1)}, /*index=5*/s32[]{:T(128)}, s32[]{:T(128)}, s32[]{:T(128)}) while((s32[]{:T(128)}, f32[384,128]{0,1:T(8,128)S(1)}, f32[384,128]{0,1:T(8,128)S(1)}, f32[384,128]{0,1:T(8,128)S(1)}, ...), condition=%wide.region_3.4_spmd, body=%wide.region_2.3_spmd.sunk | while | flops 99459 | bytes 405641 | solution.py:29
  677.8 23.3 %all_to_all.19 = bf16[32,16,384]{2,1,0:T(8,128)(2,1)S(1)} all-to-all(bf16[32,16,384]{2,1,0:T(8,128)(2,1)S(1)} %bitcast.21), channel_id=1, replica_groups=mesh['tok'=8,'row'=32] {'row'}, dimensions={0} | all-to-all | bytes 786432 | tf_op jit(solution)/shard_map/all_to_all | solution.py:88
  701.1 0.8 copy.19
  701.9 1.6 broadcast_multiply_fusion
  703.5 10.6 %subtract_convert_fusion = bf16[384,6112]{0,1:T(8,128)(2,1)} fusion(bf16[384,6112]{0,1:T(8,128)(2,1)} %param.15, bf16[256,6112]{1,0:T(8,128)(2,1)} %all-gather.2.cloned.1.call-done, f32[384,128]{0,1:T(8,128)S(1)} %get-tuple-element.305, f32[384,128]{0,1:T(8,128)S(1)} %get-tuple-element.303), kind=kOutput, calls=%fused_computation.8 | convolution fusion | flops 7217147904 | bytes 12910592 | tf_op jit(solution)/shard_map/dot_general | solution.py:75
  (1294 shorter events, 351.1 us)
Async XLA Ops:
  7.2 292.7 %copy-start.4 = (f32[8,6112]{1,0:T(8,128)S(1)}, f32[8,6112]{1,0:T(8,128)}, u32[]{:S(2)}) copy-start(f32[8,6112]{1,0:T(8,128)} %param.17) | copy-start | bytes 586756
  7.2 289.3 %all-reduce.2.cloned.1.call-start = ((), (), s32[]{:S(2)}) async-start(), calls=%async_computation.3 | async-start | bytes 524288 | tf_op jit(solution)/shard_map/psum | solution.py:12
  8.9 291.6 %slice-start = ((f32[384,256]{1,0:T(8,128)}), f32[384,128]{1,0:T(8,128)S(1)}, s32[]{:S(2)}) async-start(f32[384,256]{1,0:T(8,128)} %param.14), calls=%async_computation.5 | async-start | bytes 393216 | tf_op jit(solution)/shard_map/slice | solution.py:39
  9.0 291.8 %copy-start.3 = (s32[384,256]{1,0:T(8,128)S(1)}, s32[384,256]{1,0:T(8,128)}, u32[]{:S(2)}) copy-start(s32[384,256]{1,0:T(8,128)} %param.13) | copy-start | bytes 1179652
  9.0 692.9 %reduce-scatter.2.cloned.1.call-start = ((), (), s32[]{:S(2)}) async-start(), calls=%async_computation.4 | async-start | bytes 1769472 | tf_op jit(solution)/shard_map/reduce_scatter | solution.py:64
  299.8 1.2 copy-start.5
  299.8 188.9 %copy-start.2 = (f32[384,256]{1,0:T(8,128)S(1)}, f32[384,256]{1,0:T(8,128)}, u32[]{:S(2)}) copy-start(f32[384,256]{1,0:T(8,128)} %param.14) | copy-start | bytes 1179652
  299.8 403.7 %all-gather.2.cloned.1.call-start = ((), (), s32[]{:S(2)}) async-start(), calls=%async_computation.2 | async-start | bytes 3244032 | tf_op jit(solution)/shard_map/all_gather | solution.py:77
  301.0 376.4 %copy-start.1 = (bf16[512,256]{1,0:T(8,128)(2,1)S(1)}, bf16[512,256]{1,0:T(8,128)(2,1)}, u32[]{:S(2)}) copy-start(bf16[512,256]{1,0:T(8,128)(2,1)} %all-reduce.2.cloned.1.call-done) | copy-start | bytes 786436
  677.4 36.7 %copy-start = (f32[384,256]{1,0:T(8,128)}, f32[384,256]{1,0:T(8,128)S(1)}, u32[]{:S(2)}) copy-start(f32[384,256]{1,0:T(8,128)S(1)} %pad_maximum_fusion) | copy-start | bytes 1179652
Sparse Core Ops, SparseCore 0:
  11.2 285.2 all-reduce.1
  300.0 37.4 reduce-scatter.1
  340.3 61.0 all-gather.1
where the time goes:
time: 723 us; the launch traced here: 721 us
  waiting for transfers between devices  287 us (40%)
  other arithmetic  202 us (28%)
  local copies, waits for them, and re-layouts  168 us (23%)
  blocking collectives  23.3 us (3%)
  matrix products  14.7 us (2%)
  between operations  13.9 us (2%)
  loops' own time  12 us (2%)
    psum x1, waiting for transfers between devices, from_root(): return lax.psum(block, axis)  287 us
    div x256, other arithmetic, advance(): error_col = values * (1.0 - kept) / pivot  172 us
    dynamic_slice x256, local copies, waits for them, and re-layouts, advance(): pivot = lax.dynamic_slice_in_dim(factor_row, column, 1, 1)  151 us
    sub x256, other arithmetic, advance(): current = current - error_col * factor_row  24.9 us
    all_to_all x1, blocking collectives, on_device(): lax.all_to_all(local_outputs, 'row', split_axis=0, concat_axis=1, tiled=T...  23.3 us
  transfers between devices with their start and end apart: 3, of which 1 were waited for; matrix products, arithmetic and copies ran while one was open for 51% of the time, Pallas kernels for 0%

commit v1 on v0

v1 whole, which is shorter than its diff:
```python
import functools

import jax
import jax.numpy as jnp
from jax import lax
from jax.experimental import pallas as pl
from jax.experimental.pallas import tpu as pltpu
from jax.sharding import PartitionSpec as P

MESH = pl.DeviceIdType.MESH
F32, BF16 = jnp.float32, jnp.bfloat16

WIN = 256
BLOCK = 128
SUB = 8
LOCAL_ROWS = 384
LOCAL_TOKENS = 512
FEATURES = 1536
REST = 6112
HALF = 3072
N_ROW = 32
N_TOK = 8
CHIPS = 16
TOKENS = LOCAL_TOKENS * N_TOK

PHASES = 2
PHASE_COLS = HALF // PHASES
PIECE = PHASE_COLS // 2

Z_UP, Z_DOWN, Z_UP_PIECE, Z_DOWN_PIECE = 0, 1, 2, 3
X_FIRST = 4
PAIR_FIRST = 20
F_MESSAGES = 36


def prune_prepare(ww, kp, fw, cur, scaled_drop, fw_t):
    factor = fw[...]
    fw_t[...] = factor.T
    row_id = lax.broadcasted_iota(jnp.int32, (WIN, WIN), 0)
    col_id = lax.broadcasted_iota(jnp.int32, (WIN, WIN), 1)
    diagonal = jnp.sum(jnp.where(row_id == col_id, factor, 0.0), axis=1, keepdims=True)
    drop = (1 - kp[...]).astype(F32).T
    scaled_drop[...] = drop * (1.0 / diagonal)
    cur[...] = ww[...].T


def prune_tile(k, cur, scaled_drop, fw_t, err):
    low = k * SUB
    block_end = (low // BLOCK + 1) * BLOCK
    tile = cur[low : low + SUB, :]
    drop = scaled_drop[low : low + SUB, :]
    rows = []
    for s in range(SUB):
        e = tile[s : s + 1, :] * drop[s : s + 1, :]
        rows.append(e)
        tile = tile - fw_t[low : low + SUB, low + s : low + s + 1] * e
    cur[low : low + SUB, :] = tile
    err[low : low + SUB, :] = jnp.concatenate(rows, axis=0)
    start = low + SUB
    while start < block_end:
        end = min(start + 32, block_end)
        part = cur[start:end, :]
        for s in range(SUB):
            part = part - fw_t[start:end, low + s : low + s + 1] * rows[s]
        cur[start:end, :] = part
        start = end
    if block_end == low + SUB and block_end < WIN:
        b = block_end - BLOCK
        cur[block_end:, :] = cur[block_end:, :] - jnp.dot(
            fw_t[block_end:, b:block_end], err[b:block_end, :],
            precision=lax.Precision.HIGHEST, preferred_element_type=F32,
        )


def kernel(
    ids_hbm, calib_hbm, keep_hbm, ww_hbm, rest_hbm, fw_hbm, fr_hbm,
    pruned_out, rest_out, hess_out, outs_out,
    ids, cal, kp, ww, fw, fr, fr_split, fr_pair, fac, xin, x_t, cur, scaled_drop, err, fw_t, err_half, local_outs,
    gram, gram_half, relay_in, relay_out, from_left, from_right, peer_out, peer_in,
    load_sem, pair_sem, f_send, f_recv, scat_send, scat_recv, xz_send, xz_recv, xx_send, xx_recv, xp_sem,
    o_send, o_recv, h_send, h_recv,
):
    tok, row = lax.axis_index("tok"), lax.axis_index("row")
    x, h, c = row // 8, (row // 2) % 4, row % 2
    l, y = tok // 4, tok % 4
    chip = x * 4 + h

    def row_of(px, ph, pc):
        return ((px + 4) % 4) * 8 + ((ph + 4) % 4) * 2 + pc

    def remote(src, dst, ssem, rsem, to_row=None, to_tok=None):
        return pltpu.make_async_remote_copy(
            src_ref=src, dst_ref=dst, send_sem=ssem, recv_sem=rsem,
            device_id=(tok if to_tok is None else to_tok, row if to_row is None else to_row),
            device_id_type=MESH,
        )

    loads = [
        pltpu.make_async_copy(s, d, load_sem.at[i])
        for i, (s, d) in enumerate(
            [(fr_hbm, fr), (calib_hbm, cal), (ww_hbm, ww), (keep_hbm, kp), (fw_hbm, fw), (ids_hbm, ids), (rest_hbm, rest_out)]
        )
    ]
    for load in loads:
        load.start()

    barrier = pltpu.get_barrier_semaphore()

    def greet(d, carry):
        pl.semaphore_signal(barrier, inc=1, device_id=(tok, (row + d) % N_ROW), device_id_type=MESH)
        return carry

    lax.fori_loop(1, N_ROW, greet, 0)
    up_tok, down_tok, other_tok = l * 4 + (y + 1) % 4, l * 4 + (y + 3) % 4, (1 - l) * 4 + y
    for peer in (up_tok, down_tok, other_tok):
        pl.semaphore_signal(barrier, inc=1, device_id=(peer, row), device_id_type=MESH)
    pl.semaphore_wait(barrier, N_ROW - 1 + 3)

    is_source = row == 0
    loads[1].wait()

    def scatter(r):
        first = pl.multiple_of((r % 2) * 256 + (r // 2) * 16, 16)
        return remote(
            cal.at[pl.ds(first, 16), pl.ds(0, WIN)], xin.at[r % 2, r // 2], scat_send.at[r], scat_recv.at[0], to_row=r
        )

    @pl.when(is_source)
    def _():
        def send(r, carry):
            scatter(r).start()
            return carry

        lax.fori_loop(1, N_ROW, send, 0)
        xin[0, 0] = cal[0:16, 0:WIN]

    loads[0].wait()
    fr_split[0] = fr[:, 0:HALF]
    fr_split[1, :, HALF - 128 :] = jnp.zeros((8, 128), F32)
    fr_split[1, :, 0 : REST - HALF] = fr[:, HALF:REST]
    own_rows = pl.ds(pl.multiple_of(c * 8, 8), 8)
    pair_copy = remote(
        fr_split.at[1 - c], fr_pair.at[own_rows], pair_sem.at[0], pair_sem.at[1], to_row=row_of(x, h, 1 - c)
    )
    pair_copy.start()
    fr_pair[own_rows, :] = fr_split[c]

    for i in (2, 3, 4):
        loads[i].wait()
    prune_prepare(ww, kp, fw, cur, scaled_drop, fw_t)

    def f_copy(p, number, slot, to_row, piece=None):
        first, size = p * PHASE_COLS, PHASE_COLS
        if piece is not None:
            first, size = first + piece * PIECE, PIECE
        ref = fac.at[c, slot, :, pl.ds(first, size)]
        return remote(ref, ref, f_send.at[p, number], f_recv.at[p, number], to_row=to_row)

    x_up, x_down = row_of(x + 1, h, c), row_of(x - 1, h, c)
    z_up, z_down = row_of(x, h + 1, c), row_of(x, h - 1, c)
    pair = row_of(x, h, 1 - c)
    z_slots = [h, (h + 3) % 4, (h + 1) % 4, (h + 2) % 4]
    x_slots = [x, (x + 3) % 4, (x + 1) % 4, (x + 2) % 4]
    f_started = []

    def f_start(*args, **kw):
        copy = f_copy(*args, **kw)
        copy.start()
        f_started.append(copy)

    def f_from_z(p, j):
        slot = x * 4 + z_slots[j]
        if j == 1:
            f_start(p, Z_UP_PIECE, slot, z_up, piece=0)
        if j == 2:
            f_start(p, Z_DOWN_PIECE, slot, z_down, piece=1)
        f_start(p, X_FIRST + 4 * j, slot, x_up)
        f_start(p, X_FIRST + 4 * j + 1, slot, x_down)
        f_start(p, PAIR_FIRST + j, slot, pair)

    def f_own(p):
        f_start(p, Z_UP, chip, z_up)
        f_start(p, Z_DOWN, chip, z_down)
        f_from_z(p, 0)

    def f_z_neighbours(p):
        f_copy(p, Z_UP, x * 4 + z_slots[1], z_up).wait_recv()
        f_from_z(p, 1)
        f_copy(p, Z_DOWN, x * 4 + z_slots[2], z_down).wait_recv()
        f_from_z(p, 2)

    def f_z_opposite(p):
        slot = x * 4 + z_slots[3]
        f_copy(p, Z_UP_PIECE, slot, z_up, piece=0).wait_recv()
        f_copy(p, Z_DOWN_PIECE, slot, z_down, piece=1).wait_recv()
        f_from_z(p, 3)

    def f_x_neighbours(p, j):
        n = X_FIRST + 4 * j
        slot = x_slots[1] * 4 + z_slots[j]
        f_copy(p, n, slot, x_up).wait_recv()
        f_start(p, n + 2, slot, x_up, piece=0)
        f_start(p, PAIR_FIRST + 4 + j, slot, pair)
        slot = x_slots[2] * 4 + z_slots[j]
        f_copy(p, n + 1, slot, x_down).wait_recv()
        f_start(p, n + 3, slot, x_down, piece=1)
        f_start(p, PAIR_FIRST + 8 + j, slot, pair)

    def f_x_opposite(p, j):
        n = X_FIRST + 4 * j
        slot = x_slots[3] * 4 + z_slots[j]
        f_copy(p, n + 2, slot, x_up, piece=0).wait_recv()
        f_copy(p, n + 3, slot, x_down, piece=1).wait_recv()
        f_start(p, PAIR_FIRST + 12 + j, slot, pair)

    def f_pair_wait(p):
        for i in range(4):
            for j in range(4):
                slot = x_slots[i] * 4 + z_slots[j]
                ref = fac.at[1 - c, slot, :, pl.ds(p * PHASE_COLS, PHASE_COLS)]
                number = PAIR_FIRST + 4 * i + j
                remote(ref, ref, f_send.at[p, number], f_recv.at[p, number], to_row=pair).wait_recv()

    pair_copy.wait_recv()
    fac[c, chip] = fr_pair[...].astype(BF16)

    def xz_copy(d):
        ref = xin.at[c, chip]
        return remote(ref, ref, xz_send.at[d], xz_recv.at[d], to_row=row_of(x, h + d, c))

    @pl.when(jnp.logical_not(is_source))
    def _():
        remote(xin.at[c, chip], xin.at[c, chip], scat_send.at[0], scat_recv.at[0], to_row=row_of(x, h, 1 - c)).wait_recv()

    for d in (1, 3, 2):
        xz_copy(d).start()
    for p in range(PHASES):
        f_own(p)

    prune = functools.partial(prune_tile, cur=cur, scaled_drop=scaled_drop, fw_t=fw_t, err=err)
    for k in range(0, 8):
        prune(k)

    def xx_copy(d):
        ref = xin.at[c, pl.ds(x * 4, 4)]
        return remote(ref, ref, xx_send.at[d], xx_recv.at[d], to_row=row_of(x + d, h, c))

    for d in (1, 3, 2):
        ref = xin.at[c, x * 4 + (h + 4 - d) % 4]
        remote(ref, ref, xz_send.at[d], xz_recv.at[d], to_row=row_of(x, h + d, c)).wait_recv()
    for d in (1, 3, 2):
        xx_copy(d).start()
    for p in range(PHASES):
        f_z_neighbours(p)

    for k in range(8, 16):
        prune(k)

    for d in (1, 3, 2):
        ref = xin.at[c, pl.ds(((x + 4 - d) % 4) * 4, 4)]
        remote(ref, ref, xx_send.at[d], xx_recv.at[d], to_row=row_of(x + d, h, c)).wait_recv()
    xp_copy = remote(xin.at[c], xin.at[c], xp_sem.at[0], xp_sem.at[1], to_row=pair)
    xp_copy.start()
    for p in range(PHASES):
        f_z_opposite(p)

    for k in range(16, 24):
        prune(k)

    remote(xin.at[1 - c], xin.at[1 - c], xp_sem.at[0], xp_sem.at[1], to_row=pair).wait_recv()

    loads[5].wait()
    live = jnp.where(ids[...] != 1, 1.0, 0.0)
    live_t = jnp.concatenate([live, jnp.zeros((4, 128), F32)], axis=0).T
    x_parts = []
    for s in range(4):
        part = xin[s // 2, (s % 2) * 8 : (s % 2) * 8 + 8].reshape(128, WIN).astype(F32)
        x_parts.append(part * live_t[:, s : s + 1])
    x_all = jnp.concatenate(x_parts, axis=0)
    x_t[...] = x_all.T.astype(BF16)

    @pl.loop(0, FEATURES // 256)
    def _(i):
        cols = pl.ds(pl.multiple_of(i * 256, 256), 256)
        part = jnp.dot(x_t[...], cal[:, cols], preferred_element_type=F32).reshape(N_TOK, 32, 256)
        gram[:, :, cols] = part
        gram_half[:, :, cols] = part.astype(BF16)

    def h_copy(number, src, dst, to_tok):
        return remote(src, dst, h_send.at[number], h_recv.at[number], to_tok=to_tok)

    h_copies = [
        h_copy(0, gram_half.at[(y + 2) % 4], relay_in.at[0], up_tok),
        h_copy(1, gram_half.at[4 + (y + 2) % 4], relay_in.at[1], down_tok),
        h_copy(2, gram_half.at[4 + (y + 1) % 4], from_left.at[1], up_tok),
        h_copy(3, gram_half.at[(y + 3) % 4], from_right.at[0], down_tok),
        h_copy(4, relay_out.at[0], from_left.at[0], up_tok),
        h_copy(5, relay_out.at[1], from_right.at[1], down_tok),
        h_copy(6, peer_out, peer_in, other_tok),
    ]
    for i in range(4):
        h_copies[i].start()

    for k in range(24, 32):
        prune(k)

    pruned_t = cur[...]
    pruned_half = pruned_t.astype(BF16)
    local_outs[...] = jnp.dot(x_all.astype(BF16), pruned_half, preferred_element_type=F32).astype(BF16).reshape(N_ROW, 16, LOCAL_ROWS)

    def out_copy(d, sender, owner):
        cols = pl.ds(pl.multiple_of(sender * LOCAL_ROWS, 128), LOCAL_ROWS)
        return remote(local_outs.at[owner], outs_out.at[:, cols], o_send.at[d], o_recv.at[d], to_row=owner)

    def send_out(d, carry):
        out_copy(d, row, (row + d) % N_ROW).start()
        return carry

    lax.fori_loop(1, N_ROW, send_out, 0)

    h_copies[0].wait_recv()
    relay_out[0] = (relay_in[0].astype(F32) + gram[(y + 1) % 4]).astype(BF16)
    h_copies[4].start()
    h_copies[1].wait_recv()
    relay_out[1] = (relay_in[1].astype(F32) + gram[4 + (y + 3) % 4]).astype(BF16)
    h_copies[5].start()

    for p in range(PHASES):
        for j in range(4):
            f_x_neighbours(p, j)

    outs_out[:, pl.ds(pl.multiple_of(row * LOCAL_ROWS, 128), LOCAL_ROWS)] = local_outs[row]
    pruned_out[...] = pruned_t.T
    err_half[...] = err[...].astype(BF16)

    for i in range(2, 6):
        h_copies[i].wait_recv()
    peer_out[...] = (
        gram[(1 - l) * 4 + y] + from_left[1 - l].astype(F32) + from_right[1 - l].astype(F32)
    ).astype(BF16)
    h_copies[6].start()

    def update(half, first, size):
        factor = fac[half, :, :, pl.ds(first, size)].reshape(WIN, size)
        change = lax.dot_general(
            factor, err_half[...], (((0,), (0,)), ((), ())), preferred_element_type=F32
        )
        count = min(size, REST - (half * HALF + first)) if isinstance(first, int) else size
        start = half * HALF + first
        rows = pl.ds(start if isinstance(first, int) else pl.multiple_of(start, 256), count)
        rest_out[rows, :] = (rest_out[rows, :].astype(F32) - change[:count]).astype(BF16)

    loads[6].wait()
    step = 512
    for p in range(PHASES):
        for j in range(4):
            f_x_opposite(p, j)
        f_pair_wait(p)
        for half in range(2):
            first, count = p * PHASE_COLS, PHASE_COLS // step
            ragged = half == 1 and p == PHASES - 1

            @pl.loop(0, count - 1 if ragged else count)
            def _(i, half=half, first=first):
                update(half, pl.multiple_of(first + i * step, step), step)

            if ragged:
                update(half, HALF - step, step)

    h_copies[6].wait_recv()
    total = gram[l * 4 + y] + from_left[l].astype(F32) + from_right[l].astype(F32) + peer_in[...].astype(F32)
    hess_out[...] = total * (2.0 / TOKENS)


    def take_out(d, carry):
        sender = (row + N_ROW - d) % N_ROW
        cols = pl.ds(pl.multiple_of(sender * LOCAL_ROWS, 128), LOCAL_ROWS)
        remote(local_outs.at[row], outs_out.at[:, cols], o_send.at[d], o_recv.at[d], to_row=sender).wait_recv()
        return carry

    lax.fori_loop(1, N_ROW, take_out, 0)

    def left_out(d, carry):
        out_copy(d, row, (row + d) % N_ROW).wait_send()
        return carry

    lax.fori_loop(1, N_ROW, left_out, 0)

    @pl.when(is_source)
    def _():
        def left(r, carry):
            scatter(r).wait_send()
            return carry

        lax.fori_loop(1, N_ROW, left, 0)

    pair_copy.wait_send()
    for d in (1, 3, 2):
        xz_copy(d).wait_send()
        xx_copy(d).wait_send()
    xp_copy.wait_send()
    for copy in h_copies:
        copy.wait_send()
    for copy in f_started:
        copy.wait_send()


def on_device(token_ids, calib_input, keep_mask, weight_window, weight_rest, factor_window, factor_rest):
    vmem, dma = pltpu.VMEM, pltpu.SemaphoreType.DMA
    slab = (32, FEATURES)
    pruned, rest_t, hess, outs = pl.pallas_call(
        kernel,
        out_shape=(
            jax.ShapeDtypeStruct((LOCAL_ROWS, WIN), F32),
            jax.ShapeDtypeStruct((REST, LOCAL_ROWS), BF16),
            jax.ShapeDtypeStruct(slab, F32),
            jax.ShapeDtypeStruct((16, N_ROW * LOCAL_ROWS), BF16),
        ),
        in_specs=[pl.BlockSpec(memory_space=pltpu.HBM)] * 7,
        out_specs=[pl.BlockSpec(memory_space=vmem)] * 4,
        scratch_shapes=[
            vmem((4, 128), jnp.int32),
            vmem((LOCAL_TOKENS, FEATURES), BF16),
            vmem((LOCAL_ROWS, WIN), jnp.int32),
            vmem((LOCAL_ROWS, WIN), F32),
            vmem((WIN, WIN), F32),
            vmem((8, REST), F32),
            vmem((2, 8, HALF), F32),
            vmem((16, HALF), F32),
            vmem((2, CHIPS, 16, HALF), BF16),
            vmem((2, CHIPS, 16, WIN), BF16),
            vmem((WIN, LOCAL_TOKENS), BF16),
            vmem((WIN, LOCAL_ROWS), F32),
            vmem((WIN, LOCAL_ROWS), F32),
            vmem((WIN, LOCAL_ROWS), F32),
            vmem((WIN, WIN), F32),
            vmem((WIN, LOCAL_ROWS), BF16),
            vmem((N_ROW, 16, LOCAL_ROWS), BF16),
            vmem((N_TOK,) + slab, F32),
            vmem((N_TOK,) + slab, BF16),
            vmem((2,) + slab, BF16),
            vmem((2,) + slab, BF16),
            vmem((2,) + slab, BF16),
            vmem((2,) + slab, BF16),
            vmem(slab, BF16),
            vmem(slab, BF16),
            dma((7,)),
            dma((2,)),
            dma((PHASES, F_MESSAGES)),
            dma((PHASES, F_MESSAGES)),
            dma((N_ROW,)),
            dma((1,)),
            dma((4,)),
            dma((4,)),
            dma((4,)),
            dma((4,)),
            dma((2,)),
            dma((N_ROW,)),
            dma((N_ROW,)),
            dma((7,)),
            dma((7,)),
        ],
        compiler_params=pltpu.CompilerParams(
            collective_id=0, has_side_effects=True, vmem_limit_bytes=52 * 1024 * 1024
        ),
        cost_estimate=pl.CostEstimate(flops=2_000_000_000, bytes_accessed=16_000_000, transcendentals=0),
    )(token_ids.reshape(4, 128), calib_input, keep_mask, weight_window, weight_rest.T, factor_window, factor_rest)
    return pruned, rest_t.T, hess, outs


def solution(mesh):
    return jax.shard_map(
        on_device,
        mesh=mesh,
        in_specs=(
            P("tok"),
            P("tok", "row"),
            P("row", None),
            P("row", None),
            P("row", "tok"),
            P(),
            P("row", "tok"),
        ),
        out_specs=(P("row", None), P("row", "tok"), P("tok", "row"), P(("tok", "row"), None)),
        check_vma=False,
    )
```

time: 723 us -> 66.1 us (0.09)
  waiting for transfers between devices: 287 us -> 0 us
  other arithmetic: 202 us -> 0 us
  local copies, waits for them, and re-layouts: 168 us -> 10.7 us
  Pallas kernels: 0 us -> 54.5 us
  blocking collectives: 23.3 us -> 0 us
  matrix products: 14.7 us -> 0 us
  between operations: 13.9 us -> 0.65 us
  loops' own time: 12 us -> 0 us
    psum x1 -> x0, waiting for transfers between devices: 287 us -> none  [from_root(): return lax.psum(block, axis)]
    div x256 -> x0, other arithmetic: 172 us -> none  [advance(): error_col = values * (1.0 - kept) / pivot]
    dynamic_slice x256 -> x0, local copies, waits for them, and re-layouts: 151 us -> none  [advance(): pivot = lax.dynamic_slice_in_dim(factor_row, column, 1, 1)]
    pallas_call x0 -> x1, Pallas kernels: none -> 54.5 us  [on_device(): pl.pallas_call(kernel, out_shape=(jax.ShapeDtypeStruct((LOCAL_ROWS, WIN),...]
    sub x256 -> x0, other arithmetic: 24.9 us -> none  [advance(): current = current - error_col * factor_row]
    all_to_all x1 -> x0, blocking collectives: 23.3 us -> none  [on_device(): lax.all_to_all(local_outputs, 'row', split_axis=0, concat_axis=1, tiled=T...]
    dot_general x4 -> x0, matrix products: 14.7 us -> none  [the longest x1 10.6 us: on_device(): jnp.dot(errors, lax.all_gather(factor_rest.astype(jnp.bfloat16), 'row', a...]
    dynamic_update_slice x256 -> x0, local copies, waits for them, and re-layouts: 13.5 us -> none  [advance(): errors = lax.dynamic_update_slice_in_dim(errors, error_col, column, 1)]
  transfers between devices with their start and end apart: 3 -> 0, of which waited for: 1 -> 0; matrix products, arithmetic and copies ran while one was open for 51% -> 0% of each run, Pallas kernels for 0% -> 0%
where the time goes in v1:
time: 66.1 us; the launch traced here: 65.8 us
  Pallas kernels  54.5 us (82%)
  local copies, waits for them, and re-layouts  10.7 us (16%)
    pallas_call x1, Pallas kernels, on_device(): pl.pallas_call(kernel, out_shape=(jax.ShapeDtypeStruct((LOCAL_ROWS, WIN),...  54.5 us
    unnamed x12, local copies, waits for them, and re-layouts  10.7 us

profile of v1, /device:TPU:1, one launch (start us, length us, event | category | flops | bytes accessed | tf_op | source)
XLA Modules:
  0.0 65.8 jit_solution(2551582664039652317)
XLA Ops:
  0.6 0.0 copy-start
  0.6 1.0 %copy-done = s32[384,256]{1,0:T(8,128)S(1)} copy-done((s32[384,256]{1,0:T(8,128)S(1)}, s32[384,256]{1,0:T(8,128)}, u32[]{:S(2)}) %copy-start) | copy-done | bytes 393240
  1.6 0.0 copy-start.1
  1.6 0.9 %copy-done.1 = f32[256,256]{1,0:T(8,128)S(1)} copy-done((f32[256,256]{1,0:T(8,128)S(1)}, f32[256,256]{1,0:T(8,128)}, u32[]{:S(2)}) %copy-start.1) | copy-done | bytes 262168
  2.6 0.0 copy-start.2
  2.6 0.9 %copy-done.2 = f32[8,6112]{1,0:T(8,128)S(1)} copy-done((f32[8,6112]{1,0:T(8,128)S(1)}, f32[8,6112]{1,0:T(8,128)}, u32[]{:S(2)}) %copy-start.2) | copy-done | bytes 195608
  3.5 0.0 copy-start.3
  3.5 0.7 %copy-done.3 = s32[512]{0:T(512)S(1)} copy-done((s32[512]{0:T(512)S(1)}, s32[512]{0:T(512)}, u32[]{:S(2)}) %copy-start.3) | copy-done | bytes 2072
  4.2 54.5 %shard_map.102 = (f32[384,256]{1,0:T(8,128)S(1)}, bf16[6112,384]{1,0:T(8,128)(2,1)}, f32[32,1536]{1,0:T(8,128)S(1)}, bf16[16,12288]{1,0:T(8,128)(2,1)S(1)}) custom-call(s32[4,128]{1,0:T(4,128)S(1)} %bitcast.3, bf16[512,1536]{1,0:T(8,128)(2,1)} %calib_hbm.1, s32[384,256]{1,0:T(8,128)S(1)} %copy-done, f32[384,256]{1,0:T(8,128)} %ww_hbm.1, ...), custom_call_target="tpu_custom_call" | custom-call | flops 2000000000 | bytes 16000000 | tf_op jit(solution)/shard_map/pallas_call | solution.py:411
  58.7 0.7 %copy.15 = f32[384,256]{1,0:T(8,128)} copy(f32[384,256]{1,0:T(8,128)S(1)} %get-tuple-element.16) | data formatting | bytes 786432
  59.4 5.0 %copy.16 = bf16[384,6112]{0,1:T(8,128)(2,1)} copy(bf16[384,6112]{0,1:T(8,128)(2,1)} %bitcast.5) | data formatting | bytes 9388032
  64.4 0.7 %copy.17 = f32[32,1536]{1,0:T(8,128)} copy(f32[32,1536]{1,0:T(8,128)S(1)} %get-tuple-element.18) | data formatting | bytes 393216
  65.1 0.7 %copy.18 = bf16[16,12288]{1,0:T(8,128)(2,1)} copy(bf16[16,12288]{1,0:T(8,128)(2,1)S(1)} %get-tuple-element.19) | data formatting | bytes 786432
Async XLA Ops:
  0.6 1.0 %copy-start = (s32[384,256]{1,0:T(8,128)S(1)}, s32[384,256]{1,0:T(8,128)}, u32[]{:S(2)}) copy-start(s32[384,256]{1,0:T(8,128)} %keep_hbm.1) | copy-start | bytes 1179652
  1.6 0.9 %copy-start.1 = (f32[256,256]{1,0:T(8,128)S(1)}, f32[256,256]{1,0:T(8,128)}, u32[]{:S(2)}) copy-start(f32[256,256]{1,0:T(8,128)} %fw_hbm.1) | copy-start | bytes 786436
  2.6 0.9 %copy-start.2 = (f32[8,6112]{1,0:T(8,128)S(1)}, f32[8,6112]{1,0:T(8,128)}, u32[]{:S(2)}) copy-start(f32[8,6112]{1,0:T(8,128)} %fr_hbm.1) | copy-start | bytes 586756
  3.5 0.7 %copy-start.3 = (s32[512]{0:T(512)S(1)}, s32[512]{0:T(512)}, u32[]{:S(2)}) copy-start(s32[512]{0:T(512)} %param.7) | copy-start | bytes 6148

commit v2 on v1

--- a/solution.py
+++ b/solution.py
@@ -1,5 +1,3 @@
-import functools
-
 import jax
 import jax.numpy as jnp
 from jax import lax
@@ -26,6 +24,7 @@
 PHASES = 2
 PHASE_COLS = HALF // PHASES
 PIECE = PHASE_COLS // 2
+STEP = 512
 
 Z_UP, Z_DOWN, Z_UP_PIECE, Z_DOWN_PIECE = 0, 1, 2, 3
 X_FIRST = 4
@@ -72,10 +71,17 @@
         )
 
 
+def compensate(rest, factor, err_half):
+    change = lax.dot_general(
+        factor.reshape(WIN, -1), err_half, (((0,), (0,)), ((), ())), preferred_element_type=F32
+    )
+    return (rest.astype(F32) - change[: rest.shape[0]]).astype(BF16)
+
+
 def kernel(
     ids_hbm, calib_hbm, keep_hbm, ww_hbm, rest_hbm, fw_hbm, fr_hbm,
-    pruned_out, rest_out, hess_out, outs_out,
-    ids, cal, kp, ww, fw, fr, fr_split, fr_pair, fac, xin, x_t, cur, scaled_drop, err, fw_t, err_half, local_outs,
+    pruned_out, rest_out, hess_out, outs_out, fac, err_half,
+    ids, cal, kp, ww, fw, fr, fr_split, fr_pair, xin, x_t, cur, scaled_drop, err, fw_t, local_outs,
     gram, gram_half, relay_in, relay_out, from_left, from_right, peer_out, peer_in,
     load_sem, pair_sem, f_send, f_recv, scat_send, scat_recv, xz_send, xz_recv, xx_send, xx_recv, xp_sem,
     o_send, o_recv, h_send, h_recv,
@@ -237,9 +243,11 @@
     for p in range(PHASES):
         f_own(p)
 
-    prune = functools.partial(prune_tile, cur=cur, scaled_drop=scaled_drop, fw_t=fw_t, err=err)
-    for k in range(0, 8):
-        prune(k)
+    def prune(first, last):
+        for k in range(first, last):
+            prune_tile(k, cur, scaled_drop, fw_t, err)
+
+    prune(0, 6)
 
     def xx_copy(d):
         ref = xin.at[c, pl.ds(x * 4, 4)]
@@ -250,22 +258,22 @@
         remote(ref, ref, xz_send.at[d], xz_recv.at[d], to_row=row_of(x, h + d, c)).wait_recv()
     for d in (1, 3, 2):
         xx_copy(d).start()
-    for p in range(PHASES):
-        f_z_neighbours(p)
-
-    for k in range(8, 16):
-        prune(k)
+
+    prune(6, 9)
+    f_z_neighbours(0)
+    prune(9, 12)
+    f_x_neighbours(0, 0)
 
     for d in (1, 3, 2):
         ref = xin.at[c, pl.ds(((x + 4 - d) % 4) * 4, 4)]
         remote(ref, ref, xx_send.at[d], xx_recv.at[d], to_row=row_of(x + d, h, c)).wait_recv()
     xp_copy = remote(xin.at[c], xin.at[c], xp_sem.at[0], xp_sem.at[1], to_row=pair)
     xp_copy.start()
-    for p in range(PHASES):
-        f_z_opposite(p)
-
-    for k in range(16, 24):
-        prune(k)
+
+    prune(12, 15)
+    f_z_neighbours(1)
+    f_x_neighbours(1, 0)
+    prune(15, 18)
 
     remote(xin.at[1 - c], xin.at[1 - c], xp_sem.at[0], xp_sem.at[1], to_row=pair).wait_recv()
 
@@ -301,12 +309,20 @@
     for i in range(4):
         h_copies[i].start()
 
-    for k in range(24, 32):
-        prune(k)
+    f_z_opposite(0)
+    f_x_neighbours(0, 1)
+    prune(18, 23)
+    f_z_opposite(1)
+    f_x_neighbours(1, 1)
+    prune(23, 28)
+    f_x_neighbours(0, 2)
+    prune(28, 32)
 
     pruned_t = cur[...]
     pruned_half = pruned_t.astype(BF16)
-    local_outs[...] = jnp.dot(x_all.astype(BF16), pruned_half, preferred_element_type=F32).astype(BF16).reshape(N_ROW, 16, LOCAL_ROWS)
+    local_outs[...] = jnp.dot(
+        x_all.astype(BF16), pruned_half, preferred_element_type=F32
+    ).astype(BF16).reshape(N_ROW, 16, LOCAL_ROWS)
 
     def out_copy(d, sender, owner):
         cols = pl.ds(pl.multiple_of(sender * LOCAL_ROWS, 128), LOCAL_ROWS)
@@ -325,9 +341,13 @@
     relay_out[1] = (relay_in[1].astype(F32) + gram[4 + (y + 3) % 4]).astype(BF16)
     h_copies[5].start()
 
-    for p in range(PHASES):
-        for j in range(4):
-            f_x_neighbours(p, j)
+    f_x_neighbours(1, 2)
+    f_x_neighbours(0, 3)
+    f_x_opposite(0, 0)
+    f_x_opposite(0, 1)
+    f_x_neighbours(1, 3)
+    f_x_opposite(0, 2)
+    f_x_opposite(0, 3)
 
     outs_out[:, pl.ds(pl.multiple_of(row * LOCAL_ROWS, 128), LOCAL_ROWS)] = local_outs[row]
     pruned_out[...] = pruned_t.T
@@ -340,37 +360,27 @@
     ).astype(BF16)
     h_copies[6].start()
 
-    def update(half, first, size):
-        factor = fac[half, :, :, pl.ds(first, size)].reshape(WIN, size)
-        change = lax.dot_general(
-            factor, err_half[...], (((0,), (0,)), ((), ())), preferred_element_type=F32
-        )
-        count = min(size, REST - (half * HALF + first)) if isinstance(first, int) else size
-        start = half * HALF + first
-        rows = pl.ds(start if isinstance(first, int) else pl.multiple_of(start, 256), count)
-        rest_out[rows, :] = (rest_out[rows, :].astype(F32) - change[:count]).astype(BF16)
+    f_x_opposite(1, 0)
+    f_x_opposite(1, 1)
 
     loads[6].wait()
-    step = 512
-    for p in range(PHASES):
-        for j in range(4):
-            f_x_opposite(p, j)
+    for p in range(PHASES - 1):
         f_pair_wait(p)
         for half in range(2):
-            first, count = p * PHASE_COLS, PHASE_COLS // step
-            ragged = half == 1 and p == PHASES - 1
-
-            @pl.loop(0, count - 1 if ragged else count)
-            def _(i, half=half, first=first):
-                update(half, pl.multiple_of(first + i * step, step), step)
-
-            if ragged:
-                update(half, HALF - step, step)
+
+            @pl.loop(0, PHASE_COLS // STEP)
+            def _(i, half=half, p=p):
+                first = pl.multiple_of(p * PHASE_COLS + i * STEP, STEP)
+                rows = pl.ds(pl.multiple_of(half * HALF + first, STEP), STEP)
+                factor = fac[half, :, :, pl.ds(first, STEP)]
+                rest_out[rows, :] = compensate(rest_out[rows, :], factor, err_half[...])
+
+    f_x_opposite(1, 2)
+    f_x_opposite(1, 3)
 
     h_copies[6].wait_recv()
     total = gram[l * 4 + y] + from_left[l].astype(F32) + from_right[l].astype(F32) + peer_in[...].astype(F32)
     hess_out[...] = total * (2.0 / TOKENS)
-
 
     def take_out(d, carry):
         sender = (row + N_ROW - d) % N_ROW
@@ -379,6 +389,7 @@
         return carry
 
     lax.fori_loop(1, N_ROW, take_out, 0)
+    f_pair_wait(PHASES - 1)
 
     def left_out(d, carry):
         out_copy(d, row, (row + d) % N_ROW).wait_send()
@@ -405,19 +416,61 @@
         copy.wait_send()
 
 
+def finish_kernel(
+    pruned, rest, hess, outs, fac, err_half,
+    pruned_hbm, rest_hbm, hess_hbm, outs_hbm,
+    updated, sem,
+):
+    copies = [
+        pltpu.make_async_copy(pruned, pruned_hbm, sem.at[0]),
+        pltpu.make_async_copy(hess, hess_hbm, sem.at[1]),
+        pltpu.make_async_copy(outs, outs_hbm, sem.at[2]),
+    ]
+    last = HALF - PHASE_COLS
+    for half in range(2):
+        rows = pl.ds(half * HALF, last)
+        copies.append(pltpu.make_async_copy(rest.at[rows], rest_hbm.at[rows], sem.at[3 + half]))
+    for copy in copies:
+        copy.start()
+    for half in range(2):
+        for i in range(PHASE_COLS // STEP):
+            first = last + i * STEP
+            start = half * HALF + first
+            count = min(STEP, REST - start)
+            part = rest[start : start + count, :]
+            at = half * PHASE_COLS + i * STEP
+            updated[at : at + count, :] = compensate(part, fac[half, :, :, first : first + STEP], err_half[...])
+            copy = pltpu.make_async_copy(
+                updated.at[pl.ds(at, count)], rest_hbm.at[pl.ds(start, count)], sem.at[5 + half * (PHASE_COLS // STEP) + i]
+            )
+            copy.start()
+            copies.append(copy)
+    for copy in copies:
+        copy.wait()
+
+
 def on_device(token_ids, calib_input, keep_mask, weight_window, weight_rest, factor_window, factor_rest):
     vmem, dma = pltpu.VMEM, pltpu.SemaphoreType.DMA
     slab = (32, FEATURES)
-    pruned, rest_t, hess, outs = pl.pallas_call(
+    in_hbm = [
+        pltpu.with_memory_space_constraint(a, pltpu.HBM)
+        for a in (
+            token_ids.reshape(4, 128), calib_input, keep_mask, weight_window, weight_rest.T, factor_window, factor_rest
+        )
+    ]
+    shapes = [
+        ((LOCAL_ROWS, WIN), F32),
+        ((REST, LOCAL_ROWS), BF16),
+        (slab, F32),
+        ((16, N_ROW * LOCAL_ROWS), BF16),
+    ]
+    held = pl.pallas_call(
         kernel,
-        out_shape=(
-            jax.ShapeDtypeStruct((LOCAL_ROWS, WIN), F32),
-            jax.ShapeDtypeStruct((REST, LOCAL_ROWS), BF16),
-            jax.ShapeDtypeStruct(slab, F32),
-            jax.ShapeDtypeStruct((16, N_ROW * LOCAL_ROWS), BF16),
+        out_shape=tuple(
+            vmem(*s) for s in shapes + [((2, CHIPS, 16, HALF), BF16), ((WIN, LOCAL_ROWS), BF16)]
         ),
         in_specs=[pl.BlockSpec(memory_space=pltpu.HBM)] * 7,
-        out_specs=[pl.BlockSpec(memory_space=vmem)] * 4,
+        out_specs=[pl.BlockSpec(memory_space=vmem)] * 6,
         scratch_shapes=[
             vmem((4, 128), jnp.int32),
             vmem((LOCAL_TOKENS, FEATURES), BF16),
@@ -427,14 +480,12 @@
             vmem((8, REST), F32),
             vmem((2, 8, HALF), F32),
             vmem((16, HALF), F32),
-            vmem((2, CHIPS, 16, HALF), BF16),
             vmem((2, CHIPS, 16, WIN), BF16),
             vmem((WIN, LOCAL_TOKENS), BF16),
             vmem((WIN, LOCAL_ROWS), F32),
             vmem((WIN, LOCAL_ROWS), F32),
             vmem((WIN, LOCAL_ROWS), F32),
             vmem((WIN, WIN), F32),
-            vmem((WIN, LOCAL_ROWS), BF16),
             vmem((N_ROW, 16, LOCAL_ROWS), BF16),
             vmem((N_TOK,) + slab, F32),
             vmem((N_TOK,) + slab, BF16),
@@ -461,10 +512,22 @@
             dma((7,)),
         ],
         compiler_params=pltpu.CompilerParams(
-            collective_id=0, has_side_effects=True, vmem_limit_bytes=52 * 1024 * 1024
+            collective_id=0, has_side_effects=True, vmem_limit_bytes=32 * 1024 * 1024
         ),
         cost_estimate=pl.CostEstimate(flops=2_000_000_000, bytes_accessed=16_000_000, transcendentals=0),
-    )(token_ids.reshape(4, 128), calib_input, keep_mask, weight_window, weight_rest.T, factor_window, factor_rest)
+    )(*in_hbm)
+    pruned, rest_t, hess, outs = pl.pallas_call(
+        finish_kernel,
+        out_shape=tuple(jax.ShapeDtypeStruct(*s) for s in shapes),
+        in_specs=[pl.BlockSpec(memory_space=vmem)] * 6,
+        out_specs=[pl.BlockSpec(memory_space=pltpu.HBM)] * 4,
+        scratch_shapes=[
+            vmem((2 * PHASE_COLS, LOCAL_ROWS), BF16),
+            dma((5 + 2 * (PHASE_COLS // STEP),)),
+        ],
+        compiler_params=pltpu.CompilerParams(vmem_limit_bytes=32 * 1024 * 1024),
+        cost_estimate=pl.CostEstimate(flops=600_000_000, bytes_accessed=12_000_000, transcendentals=0),
+    )(*[pltpu.with_memory_space_constraint(a, vmem) for a in held])
     return pruned, rest_t.T, hess, outs
 
 

time: 66.1 us -> 51.5 us (0.78)
  local copies, waits for them, and re-layouts: 10.7 us -> 0 us
  Pallas kernels: 54.5 us -> 50.7 us
    unnamed x12 -> x0, local copies, waits for them, and re-layouts: 10.7 us -> none
    pallas_call x1 -> x2, Pallas kernels: 54.5 us -> 50.7 us  [the longest x1 48.2 us: on_device(): pl.pallas_call(kernel, out_shape=tuple((vmem(*s) for s in shapes + [((2,...]
where the time goes in v2:
time: 51.5 us; the launch traced here: 51.4 us
  Pallas kernels  50.7 us (98%)
  between operations  0.64 us (1%)
    pallas_call x1, Pallas kernels, on_device(): pl.pallas_call(kernel, out_shape=tuple((vmem(*s) for s in shapes + [((2,...  48.2 us
    pallas_call x1, Pallas kernels, on_device(): pl.pallas_call(finish_kernel, out_shape=tuple((jax.ShapeDtypeStruct(*s) f...  2.56 us

profile of v2, /device:TPU:1, one launch (start us, length us, event | category | flops | bytes accessed | tf_op | source)
XLA Modules:
  0.0 51.4 jit_solution(10407094950997941651)
XLA Ops:
  0.6 48.2 %shard_map.102 = (f32[384,256]{1,0:T(8,128)S(1)}, bf16[6112,384]{1,0:T(8,128)(2,1)S(1)}, f32[32,1536]{1,0:T(8,128)S(1)}, bf16[16,12288]{1,0:T(8,128)(2,1)S(1)}, ...) custom-call(s32[4,128]{1,0:T(4,128)} %bitcast.4, bf16[512,1536]{1,0:T(8,128)(2,1)} %calib_hbm.1, ...), custom_call_target="tpu_custom_call" | custom-call | flops 2000000000 | bytes 16000000 | tf_op jit(solution)/shard_map/pallas_call | solution.py:467
  48.8 2.6 %shard_map.103 = (f32[384,256]{1,0:T(8,128)}, bf16[6112,384]{1,0:T(8,128)(2,1)}, f32[32,1536]{1,0:T(8,128)}, bf16[16,12288]{1,0:T(8,128)(2,1)}) custom-call(f32[384,256]{1,0:T(8,128)S(1)} %get-tuple-element.14.pruned, bf16[6112,384]{1,0:T(8,128)(2,1)S(1)} %get-tuple-element.15.rest, f32[32,1536]{1,0:T(8,128)S(1)} %get-tuple-element.16.hess, ...), custom_call_target="tpu_custom_call" | custom-call | flops 600000000 | bytes 12000000 | tf_op jit(solution)/shard_map/pallas_call | solution.py:519

commit v3 on v2

--- a/solution.py
+++ b/solution.py
@@ -29,7 +29,7 @@
 Z_UP, Z_DOWN, Z_UP_PIECE, Z_DOWN_PIECE = 0, 1, 2, 3
 X_FIRST = 4
 PAIR_FIRST = 20
-F_MESSAGES = 36
+F_MESSAGES = 20
 
 
 def prune_prepare(ww, kp, fw, cur, scaled_drop, fw_t):
@@ -81,10 +81,10 @@
 def kernel(
     ids_hbm, calib_hbm, keep_hbm, ww_hbm, rest_hbm, fw_hbm, fr_hbm,
     pruned_out, rest_out, hess_out, outs_out, fac, err_half,
-    ids, cal, kp, ww, fw, fr, fr_split, fr_pair, xin, x_t, cur, scaled_drop, err, fw_t, local_outs,
+    ids, cal, kp, ww, fw, fr, fr_split, fr_pair, xin, x_t, cur, scaled_drop, err, fw_t, x_half, local_outs, out_relay,
     gram, gram_half, relay_in, relay_out, from_left, from_right, peer_out, peer_in,
-    load_sem, pair_sem, f_send, f_recv, scat_send, scat_recv, xz_send, xz_recv, xx_send, xx_recv, xp_sem,
-    o_send, o_recv, h_send, h_recv,
+    load_sem, pair_sem, f_send, f_recv, pair_recv, scat_send, scat_recv, xz_send, xz_recv, xx_send, xx_recv, xp_sem,
+    o_send, o_recv, relay_recv, h_send, h_recv,
 ):
     tok, row = lax.axis_index("tok"), lax.axis_index("row")
     x, h, c = row // 8, (row // 2) % 4, row % 2
@@ -107,7 +107,7 @@
             [(fr_hbm, fr), (calib_hbm, cal), (ww_hbm, ww), (keep_hbm, kp), (fw_hbm, fw), (ids_hbm, ids), (rest_hbm, rest_out)]
         )
     ]
-    for load in loads:
+    for load in loads[:6]:
         load.start()
 
     barrier = pltpu.get_barrier_semaphore()
@@ -123,22 +123,12 @@
     pl.semaphore_wait(barrier, N_ROW - 1 + 3)
 
     is_source = row == 0
-    loads[1].wait()
 
     def scatter(r):
         first = pl.multiple_of((r % 2) * 256 + (r // 2) * 16, 16)
         return remote(
             cal.at[pl.ds(first, 16), pl.ds(0, WIN)], xin.at[r % 2, r // 2], scat_send.at[r], scat_recv.at[0], to_row=r
         )
-
-    @pl.when(is_source)
-    def _():
-        def send(r, carry):
-            scatter(r).start()
-            return carry
-
-        lax.fori_loop(1, N_ROW, send, 0)
-        xin[0, 0] = cal[0:16, 0:WIN]
 
     loads[0].wait()
     fr_split[0] = fr[:, 0:HALF]
@@ -151,6 +141,17 @@
     pair_copy.start()
     fr_pair[own_rows, :] = fr_split[c]
 
+    loads[1].wait()
+
+    @pl.when(is_source)
+    def _():
+        def send(r, carry):
+            scatter(r).start()
+            return carry
+
+        lax.fori_loop(1, N_ROW, send, 0)
+        xin[0, 0] = cal[0:16, 0:WIN]
+
     for i in (2, 3, 4):
         loads[i].wait()
     prune_prepare(ww, kp, fw, cur, scaled_drop, fw_t)
@@ -159,20 +160,18 @@
         first, size = p * PHASE_COLS, PHASE_COLS
         if piece is not None:
             first, size = first + piece * PIECE, PIECE
-        ref = fac.at[c, slot, :, pl.ds(first, size)]
-        return remote(ref, ref, f_send.at[p, number], f_recv.at[p, number], to_row=to_row)
+        ref = fac.at[c * CHIPS + slot, :, pl.ds(first, size)]
+        rsem = pair_recv.at[p] if number >= PAIR_FIRST else f_recv.at[p, number]
+        return remote(ref, ref, f_send.at[0], rsem, to_row=to_row)
 
     x_up, x_down = row_of(x + 1, h, c), row_of(x - 1, h, c)
     z_up, z_down = row_of(x, h + 1, c), row_of(x, h - 1, c)
     pair = row_of(x, h, 1 - c)
     z_slots = [h, (h + 3) % 4, (h + 1) % 4, (h + 2) % 4]
     x_slots = [x, (x + 3) % 4, (x + 1) % 4, (x + 2) % 4]
-    f_started = []
 
     def f_start(*args, **kw):
-        copy = f_copy(*args, **kw)
-        copy.start()
-        f_started.append(copy)
+        f_copy(*args, **kw).start()
 
     def f_from_z(p, j):
         slot = x * 4 + z_slots[j]
@@ -220,15 +219,14 @@
         f_start(p, PAIR_FIRST + 12 + j, slot, pair)
 
     def f_pair_wait(p):
-        for i in range(4):
-            for j in range(4):
-                slot = x_slots[i] * 4 + z_slots[j]
-                ref = fac.at[1 - c, slot, :, pl.ds(p * PHASE_COLS, PHASE_COLS)]
-                number = PAIR_FIRST + 4 * i + j
-                remote(ref, ref, f_send.at[p, number], f_recv.at[p, number], to_row=pair).wait_recv()
+        ref = fac.at[pl.ds((1 - c) * CHIPS, CHIPS), :, pl.ds(p * PHASE_COLS, PHASE_COLS)]
+        remote(ref, ref, f_send.at[0], pair_recv.at[p], to_row=pair).wait_recv()
 
     pair_copy.wait_recv()
-    fac[c, chip] = fr_pair[...].astype(BF16)
+    fac[c * CHIPS + chip] = fr_pair[...].astype(BF16)
+
+    for p in range(PHASES):
+        f_own(p)
 
     def xz_copy(d):
         ref = xin.at[c, chip]
@@ -236,18 +234,18 @@
 
     @pl.when(jnp.logical_not(is_source))
     def _():
-        remote(xin.at[c, chip], xin.at[c, chip], scat_send.at[0], scat_recv.at[0], to_row=row_of(x, h, 1 - c)).wait_recv()
+        remote(xin.at[c, chip], xin.at[c, chip], scat_send.at[0], scat_recv.at[0], to_row=pair).wait_recv()
 
     for d in (1, 3, 2):
         xz_copy(d).start()
-    for p in range(PHASES):
-        f_own(p)
+    loads[6].start()
 
     def prune(first, last):
         for k in range(first, last):
             prune_tile(k, cur, scaled_drop, fw_t, err)
 
-    prune(0, 6)
+    prune(0, 8)
+    f_x_neighbours(0, 0)
 
     def xx_copy(d):
         ref = xin.at[c, pl.ds(x * 4, 4)]
@@ -259,10 +257,9 @@
     for d in (1, 3, 2):
         xx_copy(d).start()
 
-    prune(6, 9)
+    prune(8, 16)
     f_z_neighbours(0)
-    prune(9, 12)
-    f_x_neighbours(0, 0)
+    f_x_neighbours(1, 0)
 
     for d in (1, 3, 2):
         ref = xin.at[c, pl.ds(((x + 4 - d) % 4) * 4, 4)]
@@ -270,10 +267,9 @@
     xp_copy = remote(xin.at[c], xin.at[c], xp_sem.at[0], xp_sem.at[1], to_row=pair)
     xp_copy.start()
 
-    prune(12, 15)
+    prune(16, 22)
     f_z_neighbours(1)
-    f_x_neighbours(1, 0)
-    prune(15, 18)
+    f_x_neighbours(0, 1)
 
     remote(xin.at[1 - c], xin.at[1 - c], xp_sem.at[0], xp_sem.at[1], to_row=pair).wait_recv()
 
@@ -286,6 +282,7 @@
         x_parts.append(part * live_t[:, s : s + 1])
     x_all = jnp.concatenate(x_parts, axis=0)
     x_t[...] = x_all.T.astype(BF16)
+    x_half[...] = x_all.astype(BF16)
 
     @pl.loop(0, FEATURES // 256)
     def _(i):
@@ -309,30 +306,48 @@
     for i in range(4):
         h_copies[i].start()
 
+    prune(22, 27)
     f_z_opposite(0)
-    f_x_neighbours(0, 1)
-    prune(18, 23)
+    f_x_neighbours(0, 2)
+    prune(27, 32)
+
+    pruned_t = cur[...]
+    local_outs[...] = jnp.dot(
+        x_half[...], pruned_t.astype(BF16), preferred_element_type=F32
+    ).astype(BF16).reshape(4, 4, 2, 16, LOCAL_ROWS)
+
+    def out_cols(sender):
+        return pl.ds(pl.multiple_of(sender * LOCAL_ROWS, 128), LOCAL_ROWS)
+
+    opposite = (h + 2) % 4
+    relays = [
+        remote(local_outs.at[:, opposite, 0], out_relay.at[0], o_send.at[0], relay_recv.at[0], to_row=z_up),
+        remote(local_outs.at[:, opposite, 1], out_relay.at[1], o_send.at[0], relay_recv.at[1], to_row=z_down),
+    ]
+    for relay in relays:
+        relay.start()
+    my_cols = out_cols(row)
+    for dx in (2, 1, 3, 0):
+        for dh in (1, 3, 0):
+            for dc in (0, 1):
+                if (dx, dh, dc) != (0, 0, 0):
+                    ox, oh, oc = (x + dx) % 4, (h + dh) % 4, (c + dc) % 2
+                    remote(
+                        local_outs.at[ox, oh, oc], outs_out.at[:, my_cols], o_send.at[0], o_recv.at[0],
+                        to_row=row_of(ox, oh, oc),
+                    ).start()
+
+    def pass_on(way):
+        relays[way].wait_recv()
+        sender = row_of(x, h + (3 if way == 0 else 1), c)
+        for px in range(4):
+            remote(
+                out_relay.at[way, px], outs_out.at[:, out_cols(sender)], o_send.at[1], o_recv.at[0],
+                to_row=row_of(px, h + (1 if way == 0 else 3), way),
+            ).start()
+
     f_z_opposite(1)
     f_x_neighbours(1, 1)
-    prune(23, 28)
-    f_x_neighbours(0, 2)
-    prune(28, 32)
-
-    pruned_t = cur[...]
-    pruned_half = pruned_t.astype(BF16)
-    local_outs[...] = jnp.dot(
-        x_all.astype(BF16), pruned_half, preferred_element_type=F32
-    ).astype(BF16).reshape(N_ROW, 16, LOCAL_ROWS)
-
-    def out_copy(d, sender, owner):
-        cols = pl.ds(pl.multiple_of(sender * LOCAL_ROWS, 128), LOCAL_ROWS)
-        return remote(local_outs.at[owner], outs_out.at[:, cols], o_send.at[d], o_recv.at[d], to_row=owner)
-
-    def send_out(d, carry):
-        out_copy(d, row, (row + d) % N_ROW).start()
-        return carry
-
-    lax.fori_loop(1, N_ROW, send_out, 0)
 
     h_copies[0].wait_recv()
     relay_out[0] = (relay_in[0].astype(F32) + gram[(y + 1) % 4]).astype(BF16)
@@ -343,13 +358,15 @@
 
     f_x_neighbours(1, 2)
     f_x_neighbours(0, 3)
+    pass_on(0)
+    pass_on(1)
     f_x_opposite(0, 0)
     f_x_opposite(0, 1)
     f_x_neighbours(1, 3)
     f_x_opposite(0, 2)
-    f_x_opposite(0, 3)
-
-    outs_out[:, pl.ds(pl.multiple_of(row * LOCAL_ROWS, 128), LOCAL_ROWS)] = local_outs[row]
+    f_x_opposite(1, 0)
+
+    outs_out[:, my_cols] = local_outs[x, h, c]
     pruned_out[...] = pruned_t.T
     err_half[...] = err[...].astype(BF16)
 
@@ -360,7 +377,7 @@
     ).astype(BF16)
     h_copies[6].start()
 
-    f_x_opposite(1, 0)
+    f_x_opposite(0, 3)
     f_x_opposite(1, 1)
 
     loads[6].wait()
@@ -372,7 +389,7 @@
             def _(i, half=half, p=p):
                 first = pl.multiple_of(p * PHASE_COLS + i * STEP, STEP)
                 rows = pl.ds(pl.multiple_of(half * HALF + first, STEP), STEP)
-                factor = fac[half, :, :, pl.ds(first, STEP)]
+                factor = fac[half * CHIPS : (half + 1) * CHIPS, :, pl.ds(first, STEP)]
                 rest_out[rows, :] = compensate(rest_out[rows, :], factor, err_half[...])
 
     f_x_opposite(1, 2)
@@ -382,20 +399,12 @@
     total = gram[l * 4 + y] + from_left[l].astype(F32) + from_right[l].astype(F32) + peer_in[...].astype(F32)
     hess_out[...] = total * (2.0 / TOKENS)
 
-    def take_out(d, carry):
-        sender = (row + N_ROW - d) % N_ROW
-        cols = pl.ds(pl.multiple_of(sender * LOCAL_ROWS, 128), LOCAL_ROWS)
-        remote(local_outs.at[row], outs_out.at[:, cols], o_send.at[d], o_recv.at[d], to_row=sender).wait_recv()
-        return carry
-
-    lax.fori_loop(1, N_ROW, take_out, 0)
+    arrived = outs_out.at[:, pl.ds(0, (N_ROW - 1) * LOCAL_ROWS)]
+    remote(arrived, arrived, o_send.at[0], o_recv.at[0], to_row=pair).wait_recv()
     f_pair_wait(PHASES - 1)
 
-    def left_out(d, carry):
-        out_copy(d, row, (row + d) % N_ROW).wait_send()
-        return carry
-
-    lax.fori_loop(1, N_ROW, left_out, 0)
+    remote(arrived, arrived, o_send.at[0], o_recv.at[0], to_row=pair).wait_send()
+    remote(out_relay, out_relay, o_send.at[1], o_recv.at[0], to_row=pair).wait_send()
 
     @pl.when(is_source)
     def _():
@@ -412,8 +421,8 @@
     xp_copy.wait_send()
     for copy in h_copies:
         copy.wait_send()
-    for copy in f_started:
-        copy.wait_send()
+    sent = fac.at[pl.ds(0, 31)]
+    remote(sent, sent, f_send.at[0], pair_recv.at[0], to_row=pair).wait_send()
 
 
 def finish_kernel(
@@ -439,7 +448,9 @@
             count = min(STEP, REST - start)
             part = rest[start : start + count, :]
             at = half * PHASE_COLS + i * STEP
-            updated[at : at + count, :] = compensate(part, fac[half, :, :, first : first + STEP], err_half[...])
+            updated[at : at + count, :] = compensate(
+                part, fac[half * CHIPS : (half + 1) * CHIPS, :, first : first + STEP], err_half[...]
+            )
             copy = pltpu.make_async_copy(
                 updated.at[pl.ds(at, count)], rest_hbm.at[pl.ds(start, count)], sem.at[5 + half * (PHASE_COLS // STEP) + i]
             )
@@ -467,7 +478,7 @@
     held = pl.pallas_call(
         kernel,
         out_shape=tuple(
-            vmem(*s) for s in shapes + [((2, CHIPS, 16, HALF), BF16), ((WIN, LOCAL_ROWS), BF16)]
+            vmem(*s) for s in shapes + [((2 * CHIPS, 16, HALF), BF16), ((WIN, LOCAL_ROWS), BF16)]
         ),
         in_specs=[pl.BlockSpec(memory_space=pltpu.HBM)] * 7,
         out_specs=[pl.BlockSpec(memory_space=vmem)] * 6,
@@ -486,7 +497,9 @@
             vmem((WIN, LOCAL_ROWS), F32),
             vmem((WIN, LOCAL_ROWS), F32),
             vmem((WIN, WIN), F32),
-            vmem((N_ROW, 16, LOCAL_ROWS), BF16),
+            vmem((LOCAL_TOKENS, WIN), BF16),
+            vmem((4, 4, 2, 16, LOCAL_ROWS), BF16),
+            vmem((2, 4, 16, LOCAL_ROWS), BF16),
             vmem((N_TOK,) + slab, F32),
             vmem((N_TOK,) + slab, BF16),
             vmem((2,) + slab, BF16),
@@ -497,8 +510,9 @@
             vmem(slab, BF16),
             dma((7,)),
             dma((2,)),
+            dma((1,)),
             dma((PHASES, F_MESSAGES)),
-            dma((PHASES, F_MESSAGES)),
+            dma((PHASES,)),
             dma((N_ROW,)),
             dma((1,)),
             dma((4,)),
@@ -506,8 +520,9 @@
             dma((4,)),
             dma((4,)),
             dma((2,)),
-            dma((N_ROW,)),
-            dma((N_ROW,)),
+            dma((2,)),
+            dma((1,)),
+            dma((2,)),
             dma((7,)),
             dma((7,)),
         ],

time: 51.5 us -> 51.7 us (level)
  no operation moved by 1% of the time
where the time goes in v3:
time: 51.7 us; the launch traced here: 51.6 us
  Pallas kernels  51 us (99%)
  between operations  0.64 us (1%)
    pallas_call x1, Pallas kernels, on_device(): pl.pallas_call(kernel, out_shape=tuple((vmem(*s) for s in shapes + [((2 *...  48.4 us
    pallas_call x1, Pallas kernels, on_device(): pl.pallas_call(finish_kernel, out_shape=tuple((jax.ShapeDtypeStruct(*s) f...  2.56 us

profile of v3, /device:TPU:1, one launch (start us, length us, event | category | flops | bytes accessed | tf_op | source)
XLA Modules:
  0.0 51.6 jit_solution(4694265627727921557)
XLA Ops:
  0.6 48.4 %shard_map.102 = (f32[384,256]{1,0:T(8,128)S(1)}, bf16[6112,384]{1,0:T(8,128)(2,1)S(1)}, f32[32,1536]{1,0:T(8,128)S(1)}, bf16[16,12288]{1,0:T(8,128)(2,1)S(1)}, ...) custom-call(s32[4,128]{1,0:T(4,128)} %bitcast.4, bf16[512,1536]{1,0:T(8,128)(2,1)} %calib_hbm.1, ...), custom_call_target="tpu_custom_call" | custom-call | flops 2000000000 | bytes 16000000 | tf_op jit(solution)/shard_map/pallas_call | solution.py:478
  49.1 2.6 %shard_map.103 = (f32[384,256]{1,0:T(8,128)}, bf16[6112,384]{1,0:T(8,128)(2,1)}, f32[32,1536]{1,0:T(8,128)}, bf16[16,12288]{1,0:T(8,128)(2,1)}) custom-call(f32[384,256]{1,0:T(8,128)S(1)} %get-tuple-element.14.pruned, bf16[6112,384]{1,0:T(8,128)(2,1)S(1)} %get-tuple-element.15.rest, f32[32,1536]{1,0:T(8,128)S(1)} %get-tuple-element.16.hess, ...), custom_call_target="tpu_custom_call" | custom-call | flops 600000000 | bytes 12000000 | tf_op jit(solution)/shard_map/pallas_call | solution.py:534

commit v4 on v3

--- a/solution.py
+++ b/solution.py
@@ -43,25 +43,34 @@
     cur[...] = ww[...].T
 
 
-def prune_tile(k, cur, scaled_drop, fw_t, err):
+def prune_tile(k, cur, scaled_drop, fw_t, fw_s, err):
     low = k * SUB
     block_end = (low // BLOCK + 1) * BLOCK
+    shape = (SUB, LOCAL_ROWS)
     tile = cur[low : low + SUB, :]
     drop = scaled_drop[low : low + SUB, :]
-    rows = []
+    place = lax.broadcasted_iota(jnp.int32, shape, 0)
+    values = [jnp.broadcast_to(tile[s : s + 1, :], shape) for s in range(SUB)]
+    errors = []
+    tile_err = jnp.zeros(shape, F32)
+    tile_out = jnp.zeros(shape, F32)
     for s in range(SUB):
-        e = tile[s : s + 1, :] * drop[s : s + 1, :]
-        rows.append(e)
-        tile = tile - fw_t[low : low + SUB, low + s : low + s + 1] * e
-    cur[low : low + SUB, :] = tile
-    err[low : low + SUB, :] = jnp.concatenate(rows, axis=0)
+        e = values[s] * jnp.broadcast_to(drop[s : s + 1, :], shape)
+        for t in range(s + 1, SUB):
+            values[t] = values[t] - fw_s[low + s, low + t] * e
+        errors.append(e)
+        tile_err = jnp.where(place == s, e, tile_err)
+        tile_out = jnp.where(place == s, values[s] - fw_s[low + s, low + s] * e, tile_out)
+    cur[low : low + SUB, :] = tile_out
+    err[low : low + SUB, :] = tile_err
     start = low + SUB
     while start < block_end:
         end = min(start + 32, block_end)
-        part = cur[start:end, :]
+        n = (end - start) // SUB
+        part = cur[start:end, :].reshape(n, SUB, LOCAL_ROWS)
         for s in range(SUB):
-            part = part - fw_t[start:end, low + s : low + s + 1] * rows[s]
-        cur[start:end, :] = part
+            part = part - fw_t[start:end, low + s : low + s + 1].reshape(n, SUB, 1) * errors[s][None]
+        cur[start:end, :] = part.reshape(n * SUB, LOCAL_ROWS)
         start = end
     if block_end == low + SUB and block_end < WIN:
         b = block_end - BLOCK
@@ -81,7 +90,7 @@
 def kernel(
     ids_hbm, calib_hbm, keep_hbm, ww_hbm, rest_hbm, fw_hbm, fr_hbm,
     pruned_out, rest_out, hess_out, outs_out, fac, err_half,
-    ids, cal, kp, ww, fw, fr, fr_split, fr_pair, xin, x_t, cur, scaled_drop, err, fw_t, x_half, local_outs, out_relay,
+    ids, cal, kp, ww, fw, fw_s, fr, fr_split, fr_pair, xin, x_t, cur, scaled_drop, err, fw_t, x_half, local_outs, out_relay,
     gram, gram_half, relay_in, relay_out, from_left, from_right, peer_out, peer_in,
     load_sem, pair_sem, f_send, f_recv, pair_recv, scat_send, scat_recv, xz_send, xz_recv, xx_send, xx_recv, xp_sem,
     o_send, o_recv, relay_recv, h_send, h_recv,
@@ -104,10 +113,10 @@
     loads = [
         pltpu.make_async_copy(s, d, load_sem.at[i])
         for i, (s, d) in enumerate(
-            [(fr_hbm, fr), (calib_hbm, cal), (ww_hbm, ww), (keep_hbm, kp), (fw_hbm, fw), (ids_hbm, ids), (rest_hbm, rest_out)]
+            [(fr_hbm, fr), (calib_hbm, cal), (ww_hbm, ww), (keep_hbm, kp), (fw_hbm, fw), (ids_hbm, ids), (rest_hbm, rest_out), (fw_hbm, fw_s)]
         )
     ]
-    for load in loads[:6]:
+    for load in loads[:6] + loads[7:]:
         load.start()
 
     barrier = pltpu.get_barrier_semaphore()
@@ -152,7 +161,7 @@
         lax.fori_loop(1, N_ROW, send, 0)
         xin[0, 0] = cal[0:16, 0:WIN]
 
-    for i in (2, 3, 4):
+    for i in (2, 3, 4, 7):
         loads[i].wait()
     prune_prepare(ww, kp, fw, cur, scaled_drop, fw_t)
 
@@ -242,7 +251,7 @@
 
     def prune(first, last):
         for k in range(first, last):
-            prune_tile(k, cur, scaled_drop, fw_t, err)
+            prune_tile(k, cur, scaled_drop, fw_t, fw_s, err)
 
     prune(0, 8)
     f_x_neighbours(0, 0)
@@ -488,6 +497,7 @@
             vmem((LOCAL_ROWS, WIN), jnp.int32),
             vmem((LOCAL_ROWS, WIN), F32),
             vmem((WIN, WIN), F32),
+            pltpu.SMEM((WIN, WIN), F32),
             vmem((8, REST), F32),
             vmem((2, 8, HALF), F32),
             vmem((16, HALF), F32),
@@ -508,7 +518,7 @@
             vmem((2,) + slab, BF16),
             vmem(slab, BF16),
             vmem(slab, BF16),
-            dma((7,)),
+            dma((8,)),
             dma((2,)),
             dma((1,)),
             dma((PHASES, F_MESSAGES)),

time: 51.7 us -> 51.8 us (level)
  no operation moved by 1% of the time
where the time goes in v4:
time: 51.8 us; the launch traced here: 51.7 us
  Pallas kernels  51.1 us (99%)
  between operations  0.64 us (1%)
    pallas_call x1, Pallas kernels, on_device(): pl.pallas_call(kernel, out_shape=tuple((vmem(*s) for s in shapes + [((2 *...  48.5 us
    pallas_call x1, Pallas kernels, on_device(): pl.pallas_call(finish_kernel, out_shape=tuple((jax.ShapeDtypeStruct(*s) f...  2.56 us

profile of v4, /device:TPU:1, one launch (start us, length us, event | category | flops | bytes accessed | tf_op | source)
XLA Modules:
  0.0 51.7 jit_solution(7111241323918561708)
XLA Ops:
  0.6 48.5 %shard_map.102 = (f32[384,256]{1,0:T(8,128)S(1)}, bf16[6112,384]{1,0:T(8,128)(2,1)S(1)}, f32[32,1536]{1,0:T(8,128)S(1)}, bf16[16,12288]{1,0:T(8,128)(2,1)S(1)}, ...) custom-call(s32[4,128]{1,0:T(4,128)} %bitcast.4, bf16[512,1536]{1,0:T(8,128)(2,1)} %calib_hbm.1, ...), custom_call_target="tpu_custom_call" | custom-call | flops 2000000000 | bytes 16000000 | tf_op jit(solution)/shard_map/pallas_call | solution.py:487
  49.1 2.6 %shard_map.103 = (f32[384,256]{1,0:T(8,128)}, bf16[6112,384]{1,0:T(8,128)(2,1)}, f32[32,1536]{1,0:T(8,128)}, bf16[16,12288]{1,0:T(8,128)(2,1)}) custom-call(f32[384,256]{1,0:T(8,128)S(1)} %get-tuple-element.14.pruned, bf16[6112,384]{1,0:T(8,128)(2,1)S(1)} %get-tuple-element.15.rest, f32[32,1536]{1,0:T(8,128)S(1)} %get-tuple-element.16.hess, ...), custom_call_target="tpu_custom_call" | custom-call | flops 600000000 | bytes 12000000 | tf_op jit(solution)/shard_map/pallas_call | solution.py:544

commit v5 on v4

--- a/solution.py
+++ b/solution.py
@@ -234,71 +234,50 @@
     pair_copy.wait_recv()
     fac[c * CHIPS + chip] = fr_pair[...].astype(BF16)
 
-    for p in range(PHASES):
-        f_own(p)
-
     def xz_copy(d):
         ref = xin.at[c, chip]
         return remote(ref, ref, xz_send.at[d], xz_recv.at[d], to_row=row_of(x, h + d, c))
 
-    @pl.when(jnp.logical_not(is_source))
-    def _():
-        remote(xin.at[c, chip], xin.at[c, chip], scat_send.at[0], scat_recv.at[0], to_row=pair).wait_recv()
-
-    for d in (1, 3, 2):
-        xz_copy(d).start()
-    loads[6].start()
-
-    def prune(first, last):
-        for k in range(first, last):
-            prune_tile(k, cur, scaled_drop, fw_t, fw_s, err)
-
-    prune(0, 8)
-    f_x_neighbours(0, 0)
-
     def xx_copy(d):
         ref = xin.at[c, pl.ds(x * 4, 4)]
         return remote(ref, ref, xx_send.at[d], xx_recv.at[d], to_row=row_of(x + d, h, c))
 
-    for d in (1, 3, 2):
-        ref = xin.at[c, x * 4 + (h + 4 - d) % 4]
-        remote(ref, ref, xz_send.at[d], xz_recv.at[d], to_row=row_of(x, h + d, c)).wait_recv()
-    for d in (1, 3, 2):
-        xx_copy(d).start()
-
-    prune(8, 16)
-    f_z_neighbours(0)
-    f_x_neighbours(1, 0)
-
-    for d in (1, 3, 2):
-        ref = xin.at[c, pl.ds(((x + 4 - d) % 4) * 4, 4)]
-        remote(ref, ref, xx_send.at[d], xx_recv.at[d], to_row=row_of(x + d, h, c)).wait_recv()
     xp_copy = remote(xin.at[c], xin.at[c], xp_sem.at[0], xp_sem.at[1], to_row=pair)
-    xp_copy.start()
-
-    prune(16, 22)
-    f_z_neighbours(1)
-    f_x_neighbours(0, 1)
-
-    remote(xin.at[1 - c], xin.at[1 - c], xp_sem.at[0], xp_sem.at[1], to_row=pair).wait_recv()
-
-    loads[5].wait()
-    live = jnp.where(ids[...] != 1, 1.0, 0.0)
-    live_t = jnp.concatenate([live, jnp.zeros((4, 128), F32)], axis=0).T
-    x_parts = []
-    for s in range(4):
-        part = xin[s // 2, (s % 2) * 8 : (s % 2) * 8 + 8].reshape(128, WIN).astype(F32)
-        x_parts.append(part * live_t[:, s : s + 1])
-    x_all = jnp.concatenate(x_parts, axis=0)
-    x_t[...] = x_all.T.astype(BF16)
-    x_half[...] = x_all.astype(BF16)
-
-    @pl.loop(0, FEATURES // 256)
-    def _(i):
-        cols = pl.ds(pl.multiple_of(i * 256, 256), 256)
-        part = jnp.dot(x_t[...], cal[:, cols], preferred_element_type=F32).reshape(N_TOK, 32, 256)
-        gram[:, :, cols] = part
-        gram_half[:, :, cols] = part.astype(BF16)
+
+    def inputs_along_z():
+        @pl.when(jnp.logical_not(is_source))
+        def _():
+            ref = xin.at[c, chip]
+            remote(ref, ref, scat_send.at[0], scat_recv.at[0], to_row=pair).wait_recv()
+
+        for d in (1, 3, 2):
+            xz_copy(d).start()
+
+    def inputs_along_x():
+        for d in (1, 3, 2):
+            ref = xin.at[c, x * 4 + (h + 4 - d) % 4]
+            remote(ref, ref, xz_send.at[d], xz_recv.at[d], to_row=row_of(x, h + d, c)).wait_recv()
+        for d in (1, 3, 2):
+            xx_copy(d).start()
+
+    def inputs_to_pair():
+        for d in (1, 3, 2):
+            ref = xin.at[c, pl.ds(((x + 4 - d) % 4) * 4, 4)]
+            remote(ref, ref, xx_send.at[d], xx_recv.at[d], to_row=row_of(x + d, h, c)).wait_recv()
+        xp_copy.start()
+
+    def inputs_complete():
+        remote(xin.at[1 - c], xin.at[1 - c], xp_sem.at[0], xp_sem.at[1], to_row=pair).wait_recv()
+        loads[5].wait()
+        live = jnp.where(ids[...] != 1, 1.0, 0.0)
+        live_t = jnp.concatenate([live, jnp.zeros((4, 128), F32)], axis=0).T
+        x_parts = []
+        for s in range(4):
+            part = xin[s // 2, (s % 2) * 8 : (s % 2) * 8 + 8].reshape(128, WIN).astype(F32)
+            x_parts.append(part * live_t[:, s : s + 1])
+        x_all = jnp.concatenate(x_parts, axis=0)
+        x_t[...] = x_all.T.astype(BF16)
+        x_half[...] = x_all.astype(BF16)
 
     def h_copy(number, src, dst, to_tok):
         return remote(src, dst, h_send.at[number], h_recv.at[number], to_tok=to_tok)
@@ -312,39 +291,64 @@
         h_copy(5, relay_out.at[1], from_right.at[1], down_tok),
         h_copy(6, peer_out, peer_in, other_tok),
     ]
-    for i in range(4):
-        h_copies[i].start()
-
-    prune(22, 27)
-    f_z_opposite(0)
-    f_x_neighbours(0, 2)
-    prune(27, 32)
-
-    pruned_t = cur[...]
-    local_outs[...] = jnp.dot(
-        x_half[...], pruned_t.astype(BF16), preferred_element_type=F32
-    ).astype(BF16).reshape(4, 4, 2, 16, LOCAL_ROWS)
+
+    def hessian_begin():
+        @pl.loop(0, FEATURES // 256)
+        def _(i):
+            cols = pl.ds(pl.multiple_of(i * 256, 256), 256)
+            part = jnp.dot(x_t[...], cal[:, cols], preferred_element_type=F32).reshape(N_TOK, 32, 256)
+            gram[:, :, cols] = part
+            gram_half[:, :, cols] = part.astype(BF16)
+
+        for i in range(4):
+            h_copies[i].start()
+
+    def hessian_relay():
+        h_copies[0].wait_recv()
+        relay_out[0] = (relay_in[0].astype(F32) + gram[(y + 1) % 4]).astype(BF16)
+        h_copies[4].start()
+        h_copies[1].wait_recv()
+        relay_out[1] = (relay_in[1].astype(F32) + gram[4 + (y + 3) % 4]).astype(BF16)
+        h_copies[5].start()
+
+    def hessian_peer():
+        for i in range(2, 6):
+            h_copies[i].wait_recv()
+        peer_out[...] = (
+            gram[(1 - l) * 4 + y] + from_left[1 - l].astype(F32) + from_right[1 - l].astype(F32)
+        ).astype(BF16)
+        h_copies[6].start()
+
+    def hessian_end():
+        h_copies[6].wait_recv()
+        total = gram[l * 4 + y] + from_left[l].astype(F32) + from_right[l].astype(F32) + peer_in[...].astype(F32)
+        hess_out[...] = total * (2.0 / TOKENS)
 
     def out_cols(sender):
         return pl.ds(pl.multiple_of(sender * LOCAL_ROWS, 128), LOCAL_ROWS)
 
+    my_cols = out_cols(row)
     opposite = (h + 2) % 4
     relays = [
         remote(local_outs.at[:, opposite, 0], out_relay.at[0], o_send.at[0], relay_recv.at[0], to_row=z_up),
         remote(local_outs.at[:, opposite, 1], out_relay.at[1], o_send.at[0], relay_recv.at[1], to_row=z_down),
     ]
-    for relay in relays:
-        relay.start()
-    my_cols = out_cols(row)
-    for dx in (2, 1, 3, 0):
-        for dh in (1, 3, 0):
-            for dc in (0, 1):
-                if (dx, dh, dc) != (0, 0, 0):
-                    ox, oh, oc = (x + dx) % 4, (h + dh) % 4, (c + dc) % 2
-                    remote(
-                        local_outs.at[ox, oh, oc], outs_out.at[:, my_cols], o_send.at[0], o_recv.at[0],
-                        to_row=row_of(ox, oh, oc),
-                    ).start()
+
+    def send_outputs():
+        local_outs[...] = jnp.dot(
+            x_half[...], cur[...].astype(BF16), preferred_element_type=F32
+        ).astype(BF16).reshape(4, 4, 2, 16, LOCAL_ROWS)
+        for relay in relays:
+            relay.start()
+        for dx in (2, 1, 3, 0):
+            for dh in (1, 3, 0):
+                for dc in (0, 1):
+                    if (dx, dh, dc) != (0, 0, 0):
+                        ox, oh, oc = (x + dx) % 4, (h + dh) % 4, (c + dc) % 2
+                        remote(
+                            local_outs.at[ox, oh, oc], outs_out.at[:, my_cols], o_send.at[0], o_recv.at[0],
+                            to_row=row_of(ox, oh, oc),
+                        ).start()
 
     def pass_on(way):
         relays[way].wait_recv()
@@ -355,43 +359,21 @@
                 to_row=row_of(px, h + (1 if way == 0 else 3), way),
             ).start()
 
-    f_z_opposite(1)
-    f_x_neighbours(1, 1)
-
-    h_copies[0].wait_recv()
-    relay_out[0] = (relay_in[0].astype(F32) + gram[(y + 1) % 4]).astype(BF16)
-    h_copies[4].start()
-    h_copies[1].wait_recv()
-    relay_out[1] = (relay_in[1].astype(F32) + gram[4 + (y + 3) % 4]).astype(BF16)
-    h_copies[5].start()
-
-    f_x_neighbours(1, 2)
-    f_x_neighbours(0, 3)
-    pass_on(0)
-    pass_on(1)
-    f_x_opposite(0, 0)
-    f_x_opposite(0, 1)
-    f_x_neighbours(1, 3)
-    f_x_opposite(0, 2)
-    f_x_opposite(1, 0)
-
-    outs_out[:, my_cols] = local_outs[x, h, c]
-    pruned_out[...] = pruned_t.T
-    err_half[...] = err[...].astype(BF16)
-
-    for i in range(2, 6):
-        h_copies[i].wait_recv()
-    peer_out[...] = (
-        gram[(1 - l) * 4 + y] + from_left[1 - l].astype(F32) + from_right[1 - l].astype(F32)
-    ).astype(BF16)
-    h_copies[6].start()
-
-    f_x_opposite(0, 3)
-    f_x_opposite(1, 1)
-
-    loads[6].wait()
-    for p in range(PHASES - 1):
-        f_pair_wait(p)
+    arrived = outs_out.at[:, pl.ds(0, (N_ROW - 1) * LOCAL_ROWS)]
+
+    def outputs_complete():
+        remote(arrived, arrived, o_send.at[0], o_recv.at[0], to_row=pair).wait_recv()
+
+    def prune(first, last):
+        for k in range(first, last):
+            prune_tile(k, cur, scaled_drop, fw_t, fw_s, err)
+
+    def pruned_results():
+        outs_out[:, my_cols] = local_outs[x, h, c]
+        pruned_out[...] = cur[...].T
+        err_half[...] = err[...].astype(BF16)
+
+    def update(p):
         for half in range(2):
 
             @pl.loop(0, PHASE_COLS // STEP)
@@ -401,16 +383,49 @@
                 factor = fac[half * CHIPS : (half + 1) * CHIPS, :, pl.ds(first, STEP)]
                 rest_out[rows, :] = compensate(rest_out[rows, :], factor, err_half[...])
 
+    f_own(0)
+    loads[6].start()
+    prune(0, 12)
+    inputs_along_z()
+    f_own(1)
+    prune(12, 16)
+    f_z_neighbours(0)
+    prune(16, 20)
+    inputs_along_x()
+    prune(20, 28)
+    f_z_neighbours(1)
+    f_z_opposite(0)
+    inputs_to_pair()
+    prune(28, 32)
+    f_x_neighbours(0, 1)
+    f_x_neighbours(1, 0)
+    f_z_opposite(1)
+    inputs_complete()
+    hessian_begin()
+    send_outputs()
+    f_x_neighbours(0, 2)
+    f_x_neighbours(0, 0)
+    f_x_neighbours(0, 3)
+    hessian_relay()
+    pruned_results()
+    f_x_neighbours(1, 2)
+    f_x_neighbours(1, 3)
+    f_x_neighbours(1, 1)
+    f_x_opposite(1, 0)
+    pass_on(0)
+    pass_on(1)
+    for j in (1, 2, 3, 0):
+        f_x_opposite(0, j)
+    hessian_peer()
+    f_x_opposite(1, 1)
+    f_x_opposite(1, 3)
+    f_pair_wait(0)
     f_x_opposite(1, 2)
-    f_x_opposite(1, 3)
-
-    h_copies[6].wait_recv()
-    total = gram[l * 4 + y] + from_left[l].astype(F32) + from_right[l].astype(F32) + peer_in[...].astype(F32)
-    hess_out[...] = total * (2.0 / TOKENS)
-
-    arrived = outs_out.at[:, pl.ds(0, (N_ROW - 1) * LOCAL_ROWS)]
-    remote(arrived, arrived, o_send.at[0], o_recv.at[0], to_row=pair).wait_recv()
-    f_pair_wait(PHASES - 1)
+    loads[6].wait()
+    update(0)
+    outputs_complete()
+    f_pair_wait(1)
+    hessian_end()
 
     remote(arrived, arrived, o_send.at[0], o_recv.at[0], to_row=pair).wait_send()
     remote(out_relay, out_relay, o_send.at[1], o_recv.at[0], to_row=pair).wait_send()

time: 51.8 us -> 49.9 us (0.963)
  Pallas kernels: 51.1 us -> 49.1 us
    pallas_call x1, Pallas kernels: 48.5 us -> 46.6 us  [on_device(): pl.pallas_call(kernel, out_shape=tuple((vmem(*s) for s in shapes + [((2 *...]
where the time goes in v5:
time: 49.9 us; the launch traced here: 49.8 us
  Pallas kernels  49.1 us (98%)
  between operations  0.64 us (1%)
    pallas_call x1, Pallas kernels, on_device(): pl.pallas_call(kernel, out_shape=tuple((vmem(*s) for s in shapes + [((2 *...  46.6 us
    pallas_call x1, Pallas kernels, on_device(): pl.pallas_call(finish_kernel, out_shape=tuple((jax.ShapeDtypeStruct(*s) f...  2.56 us

profile of v5, /device:TPU:1, one launch (start us, length us, event | category | flops | bytes accessed | tf_op | source)
XLA Modules:
  0.0 49.8 jit_solution(8508013353529525269)
XLA Ops:
  0.6 46.6 %shard_map.102 = (f32[384,256]{1,0:T(8,128)S(1)}, bf16[6112,384]{1,0:T(8,128)(2,1)S(1)}, f32[32,1536]{1,0:T(8,128)S(1)}, bf16[16,12288]{1,0:T(8,128)(2,1)S(1)}, ...) custom-call(s32[4,128]{1,0:T(4,128)} %bitcast.4, bf16[512,1536]{1,0:T(8,128)(2,1)} %calib_hbm.1, ...), custom_call_target="tpu_custom_call" | custom-call | flops 2000000000 | bytes 16000000 | tf_op jit(solution)/shard_map/pallas_call | solution.py:502
  47.2 2.6 %shard_map.103 = (f32[384,256]{1,0:T(8,128)}, bf16[6112,384]{1,0:T(8,128)(2,1)}, f32[32,1536]{1,0:T(8,128)}, bf16[16,12288]{1,0:T(8,128)(2,1)}) custom-call(f32[384,256]{1,0:T(8,128)S(1)} %get-tuple-element.14.pruned, bf16[6112,384]{1,0:T(8,128)(2,1)S(1)} %get-tuple-element.15.rest, f32[32,1536]{1,0:T(8,128)S(1)} %get-tuple-element.16.hess, ...), custom_call_target="tpu_custom_call" | custom-call | flops 600000000 | bytes 12000000 | tf_op jit(solution)/shard_map/pallas_call | solution.py:559

commit v6 on v5

--- a/solution.py
+++ b/solution.py
@@ -43,7 +43,7 @@
     cur[...] = ww[...].T
 
 
-def prune_tile(k, cur, scaled_drop, fw_t, fw_s, err):
+def prune_tile(k, cur, scaled_drop, fw_t, fw_s, err, err_blocks):
     low = k * SUB
     block_end = (low // BLOCK + 1) * BLOCK
     shape = (SUB, LOCAL_ROWS)
@@ -63,6 +63,8 @@
         tile_out = jnp.where(place == s, values[s] - fw_s[low + s, low + s] * e, tile_out)
     cur[low : low + SUB, :] = tile_out
     err[low : low + SUB, :] = tile_err
+    at = ((k % 2) * CHIPS + k // 2) * SUB
+    err_blocks[at : at + SUB, :] = tile_err
     start = low + SUB
     while start < block_end:
         end = min(start + 32, block_end)
@@ -80,9 +82,10 @@
         )
 
 
-def compensate(rest, factor, err_half):
+def compensate(rest, blocks, half, err_half):
+    factor = blocks[:, half * 8 : half * 8 + 8, :].reshape(WIN, blocks.shape[2])
     change = lax.dot_general(
-        factor.reshape(WIN, -1), err_half, (((0,), (0,)), ((), ())), preferred_element_type=F32
+        factor, err_half, (((0,), (0,)), ((), ())), preferred_element_type=F32
     )
     return (rest.astype(F32) - change[: rest.shape[0]]).astype(BF16)
 
@@ -90,9 +93,9 @@
 def kernel(
     ids_hbm, calib_hbm, keep_hbm, ww_hbm, rest_hbm, fw_hbm, fr_hbm,
     pruned_out, rest_out, hess_out, outs_out, fac, err_half,
-    ids, cal, kp, ww, fw, fw_s, fr, fr_split, fr_pair, xin, x_t, cur, scaled_drop, err, fw_t, x_half, local_outs, out_relay,
+    ids, cal, kp, ww, fw, fw_s, fr, fr_block, xin, x_t, cur, scaled_drop, err, err_blocks, fw_t, x_half, local_outs, z_relay, x_relay,
     gram, gram_half, relay_in, relay_out, from_left, from_right, peer_out, peer_in,
-    load_sem, pair_sem, f_send, f_recv, pair_recv, scat_send, scat_recv, xz_send, xz_recv, xx_send, xx_recv, xp_sem,
+    load_sem, f_send, f_recv, pair_recv, scat_send, scat_recv, xz_send, xz_recv, xx_send, xx_recv, xp_sem,
     o_send, o_recv, relay_recv, h_send, h_recv,
 ):
     tok, row = lax.axis_index("tok"), lax.axis_index("row")
@@ -140,30 +143,10 @@
         )
 
     loads[0].wait()
-    fr_split[0] = fr[:, 0:HALF]
-    fr_split[1, :, HALF - 128 :] = jnp.zeros((8, 128), F32)
-    fr_split[1, :, 0 : REST - HALF] = fr[:, HALF:REST]
-    own_rows = pl.ds(pl.multiple_of(c * 8, 8), 8)
-    pair_copy = remote(
-        fr_split.at[1 - c], fr_pair.at[own_rows], pair_sem.at[0], pair_sem.at[1], to_row=row_of(x, h, 1 - c)
-    )
-    pair_copy.start()
-    fr_pair[own_rows, :] = fr_split[c]
-
-    loads[1].wait()
-
-    @pl.when(is_source)
-    def _():
-        def send(r, carry):
-            scatter(r).start()
-            return carry
-
-        lax.fori_loop(1, N_ROW, send, 0)
-        xin[0, 0] = cal[0:16, 0:WIN]
-
-    for i in (2, 3, 4, 7):
-        loads[i].wait()
-    prune_prepare(ww, kp, fw, cur, scaled_drop, fw_t)
+    fr_block[0:8, :] = fr[:, 0:HALF]
+    fr_block[8:16, HALF - 128 :] = jnp.zeros((8, 128), F32)
+    fr_block[8:16, 0 : REST - HALF] = fr[:, HALF:REST]
+    fac[c * CHIPS + chip] = fr_block[...].astype(BF16)
 
     def f_copy(p, number, slot, to_row, piece=None):
         first, size = p * PHASE_COLS, PHASE_COLS
@@ -231,8 +214,16 @@
         ref = fac.at[pl.ds((1 - c) * CHIPS, CHIPS), :, pl.ds(p * PHASE_COLS, PHASE_COLS)]
         remote(ref, ref, f_send.at[0], pair_recv.at[p], to_row=pair).wait_recv()
 
-    pair_copy.wait_recv()
-    fac[c * CHIPS + chip] = fr_pair[...].astype(BF16)
+    loads[1].wait()
+
+    @pl.when(is_source)
+    def _():
+        def send(r, carry):
+            scatter(r).start()
+            return carry
+
+        lax.fori_loop(1, N_ROW, send, 0)
+        xin[0, 0] = cal[0:16, 0:WIN]
 
     def xz_copy(d):
         ref = xin.at[c, chip]
@@ -328,35 +319,49 @@
         return pl.ds(pl.multiple_of(sender * LOCAL_ROWS, 128), LOCAL_ROWS)
 
     my_cols = out_cols(row)
-    opposite = (h + 2) % 4
     relays = [
-        remote(local_outs.at[:, opposite, 0], out_relay.at[0], o_send.at[0], relay_recv.at[0], to_row=z_up),
-        remote(local_outs.at[:, opposite, 1], out_relay.at[1], o_send.at[0], relay_recv.at[1], to_row=z_down),
+        remote(local_outs.at[:, 3, 0], z_relay.at[0], o_send.at[0], relay_recv.at[0], to_row=z_up),
+        remote(local_outs.at[:, 3, 1], z_relay.at[1], o_send.at[0], relay_recv.at[1], to_row=z_down),
+        remote(local_outs.at[2, pl.ds(0, 3), 0], x_relay.at[0], o_send.at[0], relay_recv.at[2], to_row=x_up),
+        remote(local_outs.at[2, pl.ds(0, 3), 1], x_relay.at[1], o_send.at[0], relay_recv.at[3], to_row=x_down),
     ]
 
     def send_outputs():
-        local_outs[...] = jnp.dot(
+        found = jnp.dot(
             x_half[...], cur[...].astype(BF16), preferred_element_type=F32
-        ).astype(BF16).reshape(4, 4, 2, 16, LOCAL_ROWS)
+        ).astype(BF16).reshape(N_ROW, 16, LOCAL_ROWS)
+        for r in range(N_ROW):
+            local_outs[(r // 8 - x + 4) % 4, ((r // 2) % 4 - h + 5) % 4, r % 2] = found[r]
         for relay in relays:
             relay.start()
-        for dx in (2, 1, 3, 0):
-            for dh in (1, 3, 0):
+        for dx in (1, 3, 0):
+            for dh in (1, -1, 0):
                 for dc in (0, 1):
                     if (dx, dh, dc) != (0, 0, 0):
-                        ox, oh, oc = (x + dx) % 4, (h + dh) % 4, (c + dc) % 2
+                        oc = (c + dc) % 2
                         remote(
-                            local_outs.at[ox, oh, oc], outs_out.at[:, my_cols], o_send.at[0], o_recv.at[0],
-                            to_row=row_of(ox, oh, oc),
+                            local_outs.at[dx, dh + 1, oc], outs_out.at[:, my_cols], o_send.at[0], o_recv.at[0],
+                            to_row=row_of(x + dx, h + dh, oc),
                         ).start()
 
-    def pass_on(way):
+    def pass_on_z(way):
         relays[way].wait_recv()
-        sender = row_of(x, h + (3 if way == 0 else 1), c)
-        for px in range(4):
+        step = 1 if way == 0 else -1
+        sender = row_of(x, h - step, c)
+        for dx in range(4):
             remote(
-                out_relay.at[way, px], outs_out.at[:, out_cols(sender)], o_send.at[1], o_recv.at[0],
-                to_row=row_of(px, h + (1 if way == 0 else 3), way),
+                z_relay.at[way, dx], outs_out.at[:, out_cols(sender)], o_send.at[1], o_recv.at[0],
+                to_row=row_of(x + dx, h + step, way),
+            ).start()
+
+    def pass_on_x(way):
+        relays[2 + way].wait_recv()
+        step = 1 if way == 0 else -1
+        sender = row_of(x - step, h, c)
+        for dh in (-1, 0, 1):
+            remote(
+                x_relay.at[way, dh + 1], outs_out.at[:, out_cols(sender)], o_send.at[2], o_recv.at[0],
+                to_row=row_of(x + step, h + dh, way),
             ).start()
 
     arrived = outs_out.at[:, pl.ds(0, (N_ROW - 1) * LOCAL_ROWS)]
@@ -366,12 +371,12 @@
 
     def prune(first, last):
         for k in range(first, last):
-            prune_tile(k, cur, scaled_drop, fw_t, fw_s, err)
+            prune_tile(k, cur, scaled_drop, fw_t, fw_s, err, err_blocks)
 
     def pruned_results():
-        outs_out[:, my_cols] = local_outs[x, h, c]
+        outs_out[:, my_cols] = local_outs[0, 1, c]
         pruned_out[...] = cur[...].T
-        err_half[...] = err[...].astype(BF16)
+        err_half[...] = err_blocks[...].astype(BF16)
 
     def update(p):
         for half in range(2):
@@ -380,46 +385,54 @@
             def _(i, half=half, p=p):
                 first = pl.multiple_of(p * PHASE_COLS + i * STEP, STEP)
                 rows = pl.ds(pl.multiple_of(half * HALF + first, STEP), STEP)
-                factor = fac[half * CHIPS : (half + 1) * CHIPS, :, pl.ds(first, STEP)]
-                rest_out[rows, :] = compensate(rest_out[rows, :], factor, err_half[...])
+                rest_out[rows, :] = compensate(rest_out[rows, :], fac[:, :, pl.ds(first, STEP)], half, err_half[...])
 
     f_own(0)
     loads[6].start()
-    prune(0, 12)
+    for i in (2, 3, 4, 7):
+        loads[i].wait()
+    prune_prepare(ww, kp, fw, cur, scaled_drop, fw_t)
+    prune(0, 4)
     inputs_along_z()
+    prune(4, 8)
     f_own(1)
+    prune(8, 12)
+    f_z_neighbours(0)
     prune(12, 16)
-    f_z_neighbours(0)
-    prune(16, 20)
     inputs_along_x()
-    prune(20, 28)
+    prune(16, 24)
     f_z_neighbours(1)
-    f_z_opposite(0)
+    prune(24, 28)
     inputs_to_pair()
     prune(28, 32)
-    f_x_neighbours(0, 1)
-    f_x_neighbours(1, 0)
-    f_z_opposite(1)
+    f_x_neighbours(0, 0)
+    f_z_opposite(0)
+    f_x_neighbours(0, 2)
     inputs_complete()
     hessian_begin()
     send_outputs()
-    f_x_neighbours(0, 2)
-    f_x_neighbours(0, 0)
+    f_x_neighbours(1, 1)
     f_x_neighbours(0, 3)
+    pruned_results()
+    f_x_neighbours(0, 1)
+    f_z_opposite(1)
     hessian_relay()
-    pruned_results()
+    f_x_neighbours(1, 0)
+    pass_on_x(0)
+    pass_on_x(1)
+    f_x_opposite(1, 1)
+    f_x_opposite(0, 2)
     f_x_neighbours(1, 2)
     f_x_neighbours(1, 3)
-    f_x_neighbours(1, 1)
+    pass_on_z(0)
+    pass_on_z(1)
+    f_x_opposite(0, 0)
+    f_x_opposite(0, 1)
     f_x_opposite(1, 0)
-    pass_on(0)
-    pass_on(1)
-    for j in (1, 2, 3, 0):
-        f_x_opposite(0, j)
+    f_x_opposite(0, 3)
     hessian_peer()
-    f_x_opposite(1, 1)
+    f_pair_wait(0)
     f_x_opposite(1, 3)
-    f_pair_wait(0)
     f_x_opposite(1, 2)
     loads[6].wait()
     update(0)
@@ -428,7 +441,8 @@
     hessian_end()
 
     remote(arrived, arrived, o_send.at[0], o_recv.at[0], to_row=pair).wait_send()
-    remote(out_relay, out_relay, o_send.at[1], o_recv.at[0], to_row=pair).wait_send()
+    remote(z_relay, z_relay, o_send.at[1], o_recv.at[0], to_row=pair).wait_send()
+    remote(x_relay, x_relay, o_send.at[2], o_recv.at[0], to_row=pair).wait_send()
 
     @pl.when(is_source)
     def _():
@@ -438,7 +452,6 @@
 
         lax.fori_loop(1, N_ROW, left, 0)
 
-    pair_copy.wait_send()
     for d in (1, 3, 2):
         xz_copy(d).wait_send()
         xx_copy(d).wait_send()
@@ -472,9 +485,7 @@
             count = min(STEP, REST - start)
             part = rest[start : start + count, :]
             at = half * PHASE_COLS + i * STEP
-            updated[at : at + count, :] = compensate(
-                part, fac[half * CHIPS : (half + 1) * CHIPS, :, first : first + STEP], err_half[...]
-            )
+            updated[at : at + count, :] = compensate(part, fac[:, :, first : first + STEP], half, err_half[...])
             copy = pltpu.make_async_copy(
                 updated.at[pl.ds(at, count)], rest_hbm.at[pl.ds(start, count)], sem.at[5 + half * (PHASE_COLS // STEP) + i]
             )
@@ -514,10 +525,10 @@
             vmem((WIN, WIN), F32),
             pltpu.SMEM((WIN, WIN), F32),
             vmem((8, REST), F32),
-            vmem((2, 8, HALF), F32),
             vmem((16, HALF), F32),
             vmem((2, CHIPS, 16, WIN), BF16),
             vmem((WIN, LOCAL_TOKENS), BF16),
+            vmem((WIN, LOCAL_ROWS), F32),
             vmem((WIN, LOCAL_ROWS), F32),
             vmem((WIN, LOCAL_ROWS), F32),
             vmem((WIN, LOCAL_ROWS), F32),
@@ -525,6 +536,7 @@
             vmem((LOCAL_TOKENS, WIN), BF16),
             vmem((4, 4, 2, 16, LOCAL_ROWS), BF16),
             vmem((2, 4, 16, LOCAL_ROWS), BF16),
+            vmem((2, 3, 16, LOCAL_ROWS), BF16),
             vmem((N_TOK,) + slab, F32),
             vmem((N_TOK,) + slab, BF16),
             vmem((2,) + slab, BF16),
@@ -534,7 +546,6 @@
             vmem(slab, BF16),
             vmem(slab, BF16),
             dma((8,)),
-            dma((2,)),
             dma((1,)),
             dma((PHASES, F_MESSAGES)),
             dma((PHASES,)),
@@ -545,9 +556,9 @@
             dma((4,)),
             dma((4,)),
             dma((2,)),
-            dma((2,)),
+            dma((3,)),
             dma((1,)),
-            dma((2,)),
+            dma((4,)),
             dma((7,)),
             dma((7,)),
         ],

time: 49.9 us -> 50.2 us (level)
  no operation moved by 1% of the time
where the time goes in v6:
time: 50.2 us; the launch traced here: 50.1 us
  Pallas kernels  49.5 us (99%)
  between operations  0.64 us (1%)
    pallas_call x1, Pallas kernels, on_device(): pl.pallas_call(kernel, out_shape=tuple((vmem(*s) for s in shapes + [((2 *...  46.9 us
    pallas_call x1, Pallas kernels, on_device(): pl.pallas_call(finish_kernel, out_shape=tuple((jax.ShapeDtypeStruct(*s) f...  2.56 us

profile of v6, /device:TPU:1, one launch (start us, length us, event | category | flops | bytes accessed | tf_op | source)
XLA Modules:
  0.0 50.1 jit_solution(9785820569562044780)
XLA Ops:
  0.6 46.9 %shard_map.102 = (f32[384,256]{1,0:T(8,128)S(1)}, bf16[6112,384]{1,0:T(8,128)(2,1)S(1)}, f32[32,1536]{1,0:T(8,128)S(1)}, bf16[16,12288]{1,0:T(8,128)(2,1)S(1)}, ...) custom-call(s32[4,128]{1,0:T(4,128)} %bitcast.4, bf16[512,1536]{1,0:T(8,128)(2,1)} %calib_hbm.1, ...), custom_call_target="tpu_custom_call" | custom-call | flops 2000000000 | bytes 16000000 | tf_op jit(solution)/shard_map/pallas_call | solution.py:513
  47.6 2.6 %shard_map.103 = (f32[384,256]{1,0:T(8,128)}, bf16[6112,384]{1,0:T(8,128)(2,1)}, f32[32,1536]{1,0:T(8,128)}, bf16[16,12288]{1,0:T(8,128)(2,1)}) custom-call(f32[384,256]{1,0:T(8,128)S(1)} %get-tuple-element.14.pruned, bf16[6112,384]{1,0:T(8,128)(2,1)S(1)} %get-tuple-element.15.rest, f32[32,1536]{1,0:T(8,128)S(1)} %get-tuple-element.16.hess, ...), custom_call_target="tpu_custom_call" | custom-call | flops 600000000 | bytes 12000000 | tf_op jit(solution)/shard_map/pallas_call | solution.py:570

commit v7 on v6

--- a/solution.py
+++ b/solution.py
@@ -21,7 +21,7 @@
 CHIPS = 16
 TOKENS = LOCAL_TOKENS * N_TOK
 
-PHASES = 2
+PHASES = 1
 PHASE_COLS = HALF // PHASES
 PIECE = PHASE_COLS // 2
 STEP = 512
@@ -394,51 +394,37 @@
     prune_prepare(ww, kp, fw, cur, scaled_drop, fw_t)
     prune(0, 4)
     inputs_along_z()
-    prune(4, 8)
-    f_own(1)
-    prune(8, 12)
-    f_z_neighbours(0)
+    prune(4, 12)
+    f_x_neighbours(0, 0)
     prune(12, 16)
     inputs_along_x()
     prune(16, 24)
-    f_z_neighbours(1)
+    f_z_neighbours(0)
     prune(24, 28)
     inputs_to_pair()
     prune(28, 32)
-    f_x_neighbours(0, 0)
+    inputs_complete()
+    send_outputs()
+    hessian_begin()
     f_z_opposite(0)
+    f_x_opposite(0, 0)
+    f_x_neighbours(0, 1)
+    pruned_results()
+    pass_on_z(1)
     f_x_neighbours(0, 2)
-    inputs_complete()
-    hessian_begin()
-    send_outputs()
-    f_x_neighbours(1, 1)
+    pass_on_z(0)
+    hessian_relay()
     f_x_neighbours(0, 3)
-    pruned_results()
-    f_x_neighbours(0, 1)
-    f_z_opposite(1)
-    hessian_relay()
-    f_x_neighbours(1, 0)
+    pass_on_x(1)
     pass_on_x(0)
-    pass_on_x(1)
-    f_x_opposite(1, 1)
+    hessian_peer()
+    f_x_opposite(0, 1)
     f_x_opposite(0, 2)
-    f_x_neighbours(1, 2)
-    f_x_neighbours(1, 3)
-    pass_on_z(0)
-    pass_on_z(1)
-    f_x_opposite(0, 0)
-    f_x_opposite(0, 1)
-    f_x_opposite(1, 0)
     f_x_opposite(0, 3)
-    hessian_peer()
+    outputs_complete()
+    hessian_end()
     f_pair_wait(0)
-    f_x_opposite(1, 3)
-    f_x_opposite(1, 2)
     loads[6].wait()
-    update(0)
-    outputs_complete()
-    f_pair_wait(1)
-    hessian_end()
 
     remote(arrived, arrived, o_send.at[0], o_recv.at[0], to_row=pair).wait_send()
     remote(z_relay, z_relay, o_send.at[1], o_recv.at[0], to_row=pair).wait_send()
@@ -473,9 +459,10 @@
         pltpu.make_async_copy(outs, outs_hbm, sem.at[2]),
     ]
     last = HALF - PHASE_COLS
-    for half in range(2):
-        rows = pl.ds(half * HALF, last)
-        copies.append(pltpu.make_async_copy(rest.at[rows], rest_hbm.at[rows], sem.at[3 + half]))
+    if last > 0:
+        for half in range(2):
+            rows = pl.ds(half * HALF, last)
+            copies.append(pltpu.make_async_copy(rest.at[rows], rest_hbm.at[rows], sem.at[3 + half]))
     for copy in copies:
         copy.start()
     for half in range(2):

time: 50.2 us -> 50.1 us (level)
  no operation moved by 1% of the time
where the time goes in v7:
time: 50.1 us; the launch traced here: 50 us
  Pallas kernels  49.4 us (99%)
  between operations  0.64 us (1%)
    pallas_call x1, Pallas kernels, on_device(): pl.pallas_call(kernel, out_shape=tuple((vmem(*s) for s in shapes + [((2 *...  46.6 us
    pallas_call x1, Pallas kernels, on_device(): pl.pallas_call(finish_kernel, out_shape=tuple((jax.ShapeDtypeStruct(*s) f...  2.77 us

profile of v7, /device:TPU:1, one launch (start us, length us, event | category | flops | bytes accessed | tf_op | source)
XLA Modules:
  0.0 50.0 jit_solution(6873360925214572620)
XLA Ops:
  0.6 46.6 %shard_map.102 = (f32[384,256]{1,0:T(8,128)S(1)}, bf16[6112,384]{1,0:T(8,128)(2,1)S(1)}, f32[32,1536]{1,0:T(8,128)S(1)}, bf16[16,12288]{1,0:T(8,128)(2,1)S(1)}, ...) custom-call(s32[4,128]{1,0:T(4,128)} %bitcast.4, bf16[512,1536]{1,0:T(8,128)(2,1)} %calib_hbm.1, ...), custom_call_target="tpu_custom_call" | custom-call | flops 2000000000 | bytes 16000000 | tf_op jit(solution)/shard_map/pallas_call | solution.py:500
  47.3 2.8 %shard_map.103 = (f32[384,256]{1,0:T(8,128)}, bf16[6112,384]{1,0:T(8,128)(2,1)}, f32[32,1536]{1,0:T(8,128)}, bf16[16,12288]{1,0:T(8,128)(2,1)}) custom-call(f32[384,256]{1,0:T(8,128)S(1)} %get-tuple-element.14.pruned, bf16[6112,384]{1,0:T(8,128)(2,1)S(1)} %get-tuple-element.15.rest, f32[32,1536]{1,0:T(8,128)S(1)} %get-tuple-element.16.hess, ...), custom_call_target="tpu_custom_call" | custom-call | flops 600000000 | bytes 12000000 | tf_op jit(solution)/shard_map/pallas_call | solution.py:557

commit v8 on v7

--- a/solution.py
+++ b/solution.py
@@ -93,9 +93,9 @@
 def kernel(
     ids_hbm, calib_hbm, keep_hbm, ww_hbm, rest_hbm, fw_hbm, fr_hbm,
     pruned_out, rest_out, hess_out, outs_out, fac, err_half,
-    ids, cal, kp, ww, fw, fw_s, fr, fr_block, xin, x_t, cur, scaled_drop, err, err_blocks, fw_t, x_half, local_outs, z_relay, x_relay,
+    ids, cal, kp, ww, fw, fw_s, fr, fr_block, x_slabs, xin, x_t, cur, scaled_drop, err, err_blocks, fw_t, x_half, local_outs, z_relay, x_relay,
     gram, gram_half, relay_in, relay_out, from_left, from_right, peer_out, peer_in,
-    load_sem, f_send, f_recv, pair_recv, scat_send, scat_recv, xz_send, xz_recv, xx_send, xx_recv, xp_sem,
+    load_sem, half_sem, f_send, f_recv, pair_recv, scat_send, scat_recv, xz_send, xz_recv, xx_send, xx_recv, xp_sem,
     o_send, o_recv, relay_recv, h_send, h_recv,
 ):
     tok, row = lax.axis_index("tok"), lax.axis_index("row")
@@ -124,23 +124,12 @@
 
     barrier = pltpu.get_barrier_semaphore()
 
-    def greet(d, carry):
+    for d in range(1, N_ROW):
         pl.semaphore_signal(barrier, inc=1, device_id=(tok, (row + d) % N_ROW), device_id_type=MESH)
-        return carry
-
-    lax.fori_loop(1, N_ROW, greet, 0)
     up_tok, down_tok, other_tok = l * 4 + (y + 1) % 4, l * 4 + (y + 3) % 4, (1 - l) * 4 + y
     for peer in (up_tok, down_tok, other_tok):
         pl.semaphore_signal(barrier, inc=1, device_id=(peer, row), device_id_type=MESH)
     pl.semaphore_wait(barrier, N_ROW - 1 + 3)
-
-    is_source = row == 0
-
-    def scatter(r):
-        first = pl.multiple_of((r % 2) * 256 + (r // 2) * 16, 16)
-        return remote(
-            cal.at[pl.ds(first, 16), pl.ds(0, WIN)], xin.at[r % 2, r // 2], scat_send.at[r], scat_recv.at[0], to_row=r
-        )
 
     loads[0].wait()
     fr_block[0:8, :] = fr[:, 0:HALF]
@@ -214,16 +203,32 @@
         ref = fac.at[pl.ds((1 - c) * CHIPS, CHIPS), :, pl.ds(p * PHASE_COLS, PHASE_COLS)]
         remote(ref, ref, f_send.at[0], pair_recv.at[p], to_row=pair).wait_recv()
 
-    loads[1].wait()
-
-    @pl.when(is_source)
-    def _():
-        def send(r, carry):
-            scatter(r).start()
-            return carry
-
-        lax.fori_loop(1, N_ROW, send, 0)
-        xin[0, 0] = cal[0:16, 0:WIN]
+    is_source_chip = row < 2
+    half_copy = remote(cal.at[pl.ds(256, 256), pl.ds(0, WIN)], x_slabs, half_sem.at[0], half_sem.at[1], to_row=pair)
+
+    def scatter(q):
+        return remote(
+            x_slabs.at[pl.ds(q * 16, 16)], xin.at[c, q], scat_send.at[0], scat_recv.at[0],
+            to_row=(q // 4) * 8 + (q % 4) * 2 + c,
+        )
+
+    def scatter_inputs():
+        loads[1].wait()
+
+        @pl.when(row == 0)
+        def _():
+            half_copy.start()
+            x_slabs[...] = cal[0:256, 0:WIN]
+
+        @pl.when(is_source_chip)
+        def _():
+            @pl.when(row == 1)
+            def _():
+                half_copy.wait_recv()
+
+            for q in range(1, CHIPS):
+                scatter(q).start()
+            xin[c, 0] = x_slabs[0:16, :]
 
     def xz_copy(d):
         ref = xin.at[c, chip]
@@ -236,7 +241,7 @@
     xp_copy = remote(xin.at[c], xin.at[c], xp_sem.at[0], xp_sem.at[1], to_row=pair)
 
     def inputs_along_z():
-        @pl.when(jnp.logical_not(is_source))
+        @pl.when(jnp.logical_not(is_source_chip))
         def _():
             ref = xin.at[c, chip]
             remote(ref, ref, scat_send.at[0], scat_recv.at[0], to_row=pair).wait_recv()
@@ -388,6 +393,7 @@
                 rest_out[rows, :] = compensate(rest_out[rows, :], fac[:, :, pl.ds(first, STEP)], half, err_half[...])
 
     f_own(0)
+    scatter_inputs()
     loads[6].start()
     for i in (2, 3, 4, 7):
         loads[i].wait()
@@ -430,13 +436,14 @@
     remote(z_relay, z_relay, o_send.at[1], o_recv.at[0], to_row=pair).wait_send()
     remote(x_relay, x_relay, o_send.at[2], o_recv.at[0], to_row=pair).wait_send()
 
-    @pl.when(is_source)
+    @pl.when(row == 0)
     def _():
-        def left(r, carry):
-            scatter(r).wait_send()
-            return carry
-
-        lax.fori_loop(1, N_ROW, left, 0)
+        half_copy.wait_send()
+
+    @pl.when(is_source_chip)
+    def _():
+        sent = x_slabs.at[pl.ds(16, 240)]
+        remote(sent, sent, scat_send.at[0], scat_recv.at[0], to_row=pair).wait_send()
 
     for d in (1, 3, 2):
         xz_copy(d).wait_send()
@@ -513,6 +520,7 @@
             pltpu.SMEM((WIN, WIN), F32),
             vmem((8, REST), F32),
             vmem((16, HALF), F32),
+            vmem((256, WIN), BF16),
             vmem((2, CHIPS, 16, WIN), BF16),
             vmem((WIN, LOCAL_TOKENS), BF16),
             vmem((WIN, LOCAL_ROWS), F32),
@@ -533,10 +541,11 @@
             vmem(slab, BF16),
             vmem(slab, BF16),
             dma((8,)),
+            dma((2,)),
             dma((1,)),
             dma((PHASES, F_MESSAGES)),
             dma((PHASES,)),
-            dma((N_ROW,)),
+            dma((1,)),
             dma((1,)),
             dma((4,)),
             dma((4,)),

time: 50.1 us -> 51.3 us (1.024)
  Pallas kernels: 49.4 us -> 50.6 us
    pallas_call x1, Pallas kernels: 46.6 us -> 47.8 us  [on_device(): pl.pallas_call(kernel, out_shape=tuple((vmem(*s) for s in shapes + [((2 *...]
where the time goes in v8:
time: 51.3 us; the launch traced here: 51.2 us
  Pallas kernels  50.6 us (99%)
  between operations  0.64 us (1%)
    pallas_call x1, Pallas kernels, on_device(): pl.pallas_call(kernel, out_shape=tuple((vmem(*s) for s in shapes + [((2 *...  47.8 us
    pallas_call x1, Pallas kernels, on_device(): pl.pallas_call(finish_kernel, out_shape=tuple((jax.ShapeDtypeStruct(*s) f...  2.77 us

profile of v8, /device:TPU:1, one launch (start us, length us, event | category | flops | bytes accessed | tf_op | source)
XLA Modules:
  0.0 51.2 jit_solution(14465842037700844094)
XLA Ops:
  0.6 47.8 %shard_map.102 = (f32[384,256]{1,0:T(8,128)S(1)}, bf16[6112,384]{1,0:T(8,128)(2,1)S(1)}, f32[32,1536]{1,0:T(8,128)S(1)}, bf16[16,12288]{1,0:T(8,128)(2,1)S(1)}, ...) custom-call(s32[4,128]{1,0:T(4,128)} %bitcast.4, bf16[512,1536]{1,0:T(8,128)(2,1)} %calib_hbm.1, ...), custom_call_target="tpu_custom_call" | custom-call | flops 2000000000 | bytes 16000000 | tf_op jit(solution)/shard_map/pallas_call | solution.py:507
  48.4 2.8 %shard_map.103 = (f32[384,256]{1,0:T(8,128)}, bf16[6112,384]{1,0:T(8,128)(2,1)}, f32[32,1536]{1,0:T(8,128)}, bf16[16,12288]{1,0:T(8,128)(2,1)}) custom-call(f32[384,256]{1,0:T(8,128)S(1)} %get-tuple-element.14.pruned, bf16[6112,384]{1,0:T(8,128)(2,1)S(1)} %get-tuple-element.15.rest, f32[32,1536]{1,0:T(8,128)S(1)} %get-tuple-element.16.hess, ...), custom_call_target="tpu_custom_call" | custom-call | flops 600000000 | bytes 12000000 | tf_op jit(solution)/shard_map/pallas_call | solution.py:566

commit v9 on v7

--- a/solution.py
+++ b/solution.py
@@ -93,7 +93,7 @@
 def kernel(
     ids_hbm, calib_hbm, keep_hbm, ww_hbm, rest_hbm, fw_hbm, fr_hbm,
     pruned_out, rest_out, hess_out, outs_out, fac, err_half,
-    ids, cal, kp, ww, fw, fw_s, fr, fr_block, xin, x_t, cur, scaled_drop, err, err_blocks, fw_t, x_half, local_outs, z_relay, x_relay,
+    ids, cal, kp, ww, fw, fw_s, fr, fr_block, xin, x_t, cur, scaled_drop, err, err_blocks, fw_t, x_half, local_outs, z_relay,
     gram, gram_half, relay_in, relay_out, from_left, from_right, peer_out, peer_in,
     load_sem, f_send, f_recv, pair_recv, scat_send, scat_recv, xz_send, xz_recv, xx_send, xx_recv, xp_sem,
     o_send, o_recv, relay_recv, h_send, h_recv,
@@ -213,17 +213,6 @@
     def f_pair_wait(p):
         ref = fac.at[pl.ds((1 - c) * CHIPS, CHIPS), :, pl.ds(p * PHASE_COLS, PHASE_COLS)]
         remote(ref, ref, f_send.at[0], pair_recv.at[p], to_row=pair).wait_recv()
-
-    loads[1].wait()
-
-    @pl.when(is_source)
-    def _():
-        def send(r, carry):
-            scatter(r).start()
-            return carry
-
-        lax.fori_loop(1, N_ROW, send, 0)
-        xin[0, 0] = cal[0:16, 0:WIN]
 
     def xz_copy(d):
         ref = xin.at[c, chip]
@@ -319,49 +308,35 @@
         return pl.ds(pl.multiple_of(sender * LOCAL_ROWS, 128), LOCAL_ROWS)
 
     my_cols = out_cols(row)
+    opposite = (h + 2) % 4
     relays = [
-        remote(local_outs.at[:, 3, 0], z_relay.at[0], o_send.at[0], relay_recv.at[0], to_row=z_up),
-        remote(local_outs.at[:, 3, 1], z_relay.at[1], o_send.at[0], relay_recv.at[1], to_row=z_down),
-        remote(local_outs.at[2, pl.ds(0, 3), 0], x_relay.at[0], o_send.at[0], relay_recv.at[2], to_row=x_up),
-        remote(local_outs.at[2, pl.ds(0, 3), 1], x_relay.at[1], o_send.at[0], relay_recv.at[3], to_row=x_down),
+        remote(local_outs.at[:, opposite, 0], z_relay.at[0], o_send.at[0], relay_recv.at[0], to_row=z_up),
+        remote(local_outs.at[:, opposite, 1], z_relay.at[1], o_send.at[0], relay_recv.at[1], to_row=z_down),
     ]
 
     def send_outputs():
-        found = jnp.dot(
+        local_outs[...] = jnp.dot(
             x_half[...], cur[...].astype(BF16), preferred_element_type=F32
-        ).astype(BF16).reshape(N_ROW, 16, LOCAL_ROWS)
-        for r in range(N_ROW):
-            local_outs[(r // 8 - x + 4) % 4, ((r // 2) % 4 - h + 5) % 4, r % 2] = found[r]
+        ).astype(BF16).reshape(4, 4, 2, 16, LOCAL_ROWS)
         for relay in relays:
             relay.start()
-        for dx in (1, 3, 0):
-            for dh in (1, -1, 0):
+        for dx in (2, 1, 3, 0):
+            for dh in (1, 3, 0):
                 for dc in (0, 1):
                     if (dx, dh, dc) != (0, 0, 0):
-                        oc = (c + dc) % 2
+                        ox, oh, oc = (x + dx) % 4, (h + dh) % 4, (c + dc) % 2
                         remote(
-                            local_outs.at[dx, dh + 1, oc], outs_out.at[:, my_cols], o_send.at[0], o_recv.at[0],
-                            to_row=row_of(x + dx, h + dh, oc),
+                            local_outs.at[ox, oh, oc], outs_out.at[:, my_cols], o_send.at[0], o_recv.at[0],
+                            to_row=row_of(ox, oh, oc),
                         ).start()
 
     def pass_on_z(way):
         relays[way].wait_recv()
-        step = 1 if way == 0 else -1
-        sender = row_of(x, h - step, c)
-        for dx in range(4):
+        sender = row_of(x, h + (3 if way == 0 else 1), c)
+        for px in range(4):
             remote(
-                z_relay.at[way, dx], outs_out.at[:, out_cols(sender)], o_send.at[1], o_recv.at[0],
-                to_row=row_of(x + dx, h + step, way),
-            ).start()
-
-    def pass_on_x(way):
-        relays[2 + way].wait_recv()
-        step = 1 if way == 0 else -1
-        sender = row_of(x - step, h, c)
-        for dh in (-1, 0, 1):
-            remote(
-                x_relay.at[way, dh + 1], outs_out.at[:, out_cols(sender)], o_send.at[2], o_recv.at[0],
-                to_row=row_of(x + step, h + dh, way),
+                z_relay.at[way, px], outs_out.at[:, out_cols(sender)], o_send.at[1], o_recv.at[0],
+                to_row=row_of(px, h + (1 if way == 0 else 3), way),
             ).start()
 
     arrived = outs_out.at[:, pl.ds(0, (N_ROW - 1) * LOCAL_ROWS)]
@@ -374,7 +349,7 @@
             prune_tile(k, cur, scaled_drop, fw_t, fw_s, err, err_blocks)
 
     def pruned_results():
-        outs_out[:, my_cols] = local_outs[0, 1, c]
+        outs_out[:, my_cols] = local_outs[x, h, c]
         pruned_out[...] = cur[...].T
         err_half[...] = err_blocks[...].astype(BF16)
 
@@ -389,6 +364,17 @@
 
     f_own(0)
     loads[6].start()
+    loads[1].wait()
+
+    @pl.when(is_source)
+    def _():
+        def send(r, carry):
+            scatter(r).start()
+            return carry
+
+        lax.fori_loop(1, N_ROW, send, 0)
+        xin[0, 0] = cal[0:16, 0:WIN]
+
     for i in (2, 3, 4, 7):
         loads[i].wait()
     prune_prepare(ww, kp, fw, cur, scaled_drop, fw_t)
@@ -407,28 +393,25 @@
     send_outputs()
     hessian_begin()
     f_z_opposite(0)
+    f_x_neighbours(0, 2)
+    f_x_neighbours(0, 1)
+    hessian_relay()
+    pass_on_z(1)
+    pass_on_z(0)
+    f_x_neighbours(0, 3)
     f_x_opposite(0, 0)
-    f_x_neighbours(0, 1)
     pruned_results()
-    pass_on_z(1)
-    f_x_neighbours(0, 2)
-    pass_on_z(0)
-    hessian_relay()
-    f_x_neighbours(0, 3)
-    pass_on_x(1)
-    pass_on_x(0)
     hessian_peer()
+    f_x_opposite(0, 2)
     f_x_opposite(0, 1)
-    f_x_opposite(0, 2)
     f_x_opposite(0, 3)
+    loads[6].wait()
     outputs_complete()
     hessian_end()
     f_pair_wait(0)
-    loads[6].wait()
 
     remote(arrived, arrived, o_send.at[0], o_recv.at[0], to_row=pair).wait_send()
     remote(z_relay, z_relay, o_send.at[1], o_recv.at[0], to_row=pair).wait_send()
-    remote(x_relay, x_relay, o_send.at[2], o_recv.at[0], to_row=pair).wait_send()
 
     @pl.when(is_source)
     def _():
@@ -523,7 +506,6 @@
             vmem((LOCAL_TOKENS, WIN), BF16),
             vmem((4, 4, 2, 16, LOCAL_ROWS), BF16),
             vmem((2, 4, 16, LOCAL_ROWS), BF16),
-            vmem((2, 3, 16, LOCAL_ROWS), BF16),
             vmem((N_TOK,) + slab, F32),
             vmem((N_TOK,) + slab, BF16),
             vmem((2,) + slab, BF16),
@@ -543,9 +525,9 @@
             dma((4,)),
             dma((4,)),
             dma((2,)),
-            dma((3,)),
+            dma((2,)),
             dma((1,)),
-            dma((4,)),
+            dma((2,)),
             dma((7,)),
             dma((7,)),
         ],

time: 50.1 us -> 52.1 us (1.040)
  Pallas kernels: 49.4 us -> 51.4 us
    pallas_call x1, Pallas kernels: 46.6 us -> 48.6 us  [on_device(): pl.pallas_call(kernel, out_shape=tuple((vmem(*s) for s in shapes + [((2 *...]
where the time goes in v9:
time: 52.1 us; the launch traced here: 52 us
  Pallas kernels  51.4 us (99%)
  between operations  0.64 us (1%)
    pallas_call x1, Pallas kernels, on_device(): pl.pallas_call(kernel, out_shape=tuple((vmem(*s) for s in shapes + [((2 *...  48.6 us
    pallas_call x1, Pallas kernels, on_device(): pl.pallas_call(finish_kernel, out_shape=tuple((jax.ShapeDtypeStruct(*s) f...  2.77 us

profile of v9, /device:TPU:1, one launch (start us, length us, event | category | flops | bytes accessed | tf_op | source)
XLA Modules:
  0.0 52.0 jit_solution(2236706198638846947)
XLA Ops:
  0.6 48.6 %shard_map.102 = (f32[384,256]{1,0:T(8,128)S(1)}, bf16[6112,384]{1,0:T(8,128)(2,1)S(1)}, f32[32,1536]{1,0:T(8,128)S(1)}, bf16[16,12288]{1,0:T(8,128)(2,1)S(1)}, ...) custom-call(s32[4,128]{1,0:T(4,128)} %bitcast.4, bf16[512,1536]{1,0:T(8,128)(2,1)} %calib_hbm.1, ...), custom_call_target="tpu_custom_call" | custom-call | flops 2000000000 | bytes 16000000 | tf_op jit(solution)/shard_map/pallas_call | solution.py:483
  49.3 2.8 %shard_map.103 = (f32[384,256]{1,0:T(8,128)}, bf16[6112,384]{1,0:T(8,128)(2,1)}, f32[32,1536]{1,0:T(8,128)}, bf16[16,12288]{1,0:T(8,128)(2,1)}) custom-call(f32[384,256]{1,0:T(8,128)S(1)} %get-tuple-element.14.pruned, bf16[6112,384]{1,0:T(8,128)(2,1)S(1)} %get-tuple-element.15.rest, f32[32,1536]{1,0:T(8,128)S(1)} %get-tuple-element.16.hess, ...), custom_call_target="tpu_custom_call" | custom-call | flops 600000000 | bytes 12000000 | tf_op jit(solution)/shard_map/pallas_call | solution.py:539

commit v10 on v7

--- a/solution.py
+++ b/solution.py
@@ -175,10 +175,9 @@
         f_start(p, X_FIRST + 4 * j + 1, slot, x_down)
         f_start(p, PAIR_FIRST + j, slot, pair)
 
-    def f_own(p):
+    def f_own_along_z(p):
         f_start(p, Z_UP, chip, z_up)
         f_start(p, Z_DOWN, chip, z_down)
-        f_from_z(p, 0)
 
     def f_z_neighbours(p):
         f_copy(p, Z_UP, x * 4 + z_slots[1], z_up).wait_recv()
@@ -387,22 +386,21 @@
                 rows = pl.ds(pl.multiple_of(half * HALF + first, STEP), STEP)
                 rest_out[rows, :] = compensate(rest_out[rows, :], fac[:, :, pl.ds(first, STEP)], half, err_half[...])
 
-    f_own(0)
+    f_from_z(0, 0)
     loads[6].start()
     for i in (2, 3, 4, 7):
         loads[i].wait()
     prune_prepare(ww, kp, fw, cur, scaled_drop, fw_t)
     prune(0, 4)
     inputs_along_z()
+    f_own_along_z(0)
     prune(4, 12)
+    inputs_along_x()
     f_x_neighbours(0, 0)
-    prune(12, 16)
-    inputs_along_x()
-    prune(16, 24)
+    prune(12, 24)
+    inputs_to_pair()
+    prune(24, 32)
     f_z_neighbours(0)
-    prune(24, 28)
-    inputs_to_pair()
-    prune(28, 32)
     inputs_complete()
     send_outputs()
     hessian_begin()

time: 50.1 us -> 49.8 us (level); the launches traced: 50 us -> 49 us
  Pallas kernels: 49.4 us -> 48.4 us
    pallas_call x1, Pallas kernels: 46.6 us -> 45.6 us  [on_device(): pl.pallas_call(kernel, out_shape=tuple((vmem(*s) for s in shapes + [((2 *...]
where the time goes in v10:
time: 49.8 us; the launch traced here: 49 us
  Pallas kernels  48.4 us (97%)
  between operations  0.64 us (1%)
    pallas_call x1, Pallas kernels, on_device(): pl.pallas_call(kernel, out_shape=tuple((vmem(*s) for s in shapes + [((2 *...  45.6 us
    pallas_call x1, Pallas kernels, on_device(): pl.pallas_call(finish_kernel, out_shape=tuple((jax.ShapeDtypeStruct(*s) f...  2.77 us

profile of v10, /device:TPU:1, one launch (start us, length us, event | category | flops | bytes accessed | tf_op | source)
XLA Modules:
  0.0 49.0 jit_solution(13915315030385948092)
XLA Ops:
  0.6 45.6 %shard_map.102 = (f32[384,256]{1,0:T(8,128)S(1)}, bf16[6112,384]{1,0:T(8,128)(2,1)S(1)}, f32[32,1536]{1,0:T(8,128)S(1)}, bf16[16,12288]{1,0:T(8,128)(2,1)S(1)}, ...) custom-call(s32[4,128]{1,0:T(4,128)} %bitcast.4, bf16[512,1536]{1,0:T(8,128)(2,1)} %calib_hbm.1, ...), custom_call_target="tpu_custom_call" | custom-call | flops 2000000000 | bytes 16000000 | tf_op jit(solution)/shard_map/pallas_call | solution.py:498
  46.3 2.8 %shard_map.103 = (f32[384,256]{1,0:T(8,128)}, bf16[6112,384]{1,0:T(8,128)(2,1)}, f32[32,1536]{1,0:T(8,128)}, bf16[16,12288]{1,0:T(8,128)(2,1)}) custom-call(f32[384,256]{1,0:T(8,128)S(1)} %get-tuple-element.14.pruned, bf16[6112,384]{1,0:T(8,128)(2,1)S(1)} %get-tuple-element.15.rest, f32[32,1536]{1,0:T(8,128)S(1)} %get-tuple-element.16.hess, ...), custom_call_target="tpu_custom_call" | custom-call | flops 600000000 | bytes 12000000 | tf_op jit(solution)/shard_map/pallas_call | solution.py:555

commit v11 on v10

--- a/solution.py
+++ b/solution.py
@@ -391,15 +391,14 @@
     for i in (2, 3, 4, 7):
         loads[i].wait()
     prune_prepare(ww, kp, fw, cur, scaled_drop, fw_t)
-    prune(0, 4)
     inputs_along_z()
     f_own_along_z(0)
-    prune(4, 12)
+    prune(0, 10)
     inputs_along_x()
     f_x_neighbours(0, 0)
-    prune(12, 24)
+    prune(10, 22)
     inputs_to_pair()
-    prune(24, 32)
+    prune(22, 32)
     f_z_neighbours(0)
     inputs_complete()
     send_outputs()

time: 49.8 us -> 50.8 us (1.020)
  the two profiles are of different devices: /device:TPU:1 before, /device:TPU:16 now
where the time goes in v11:
time: 50.8 us; the launch traced here: 50.7 us
  Pallas kernels  50 us (98%)
  between operations  0.64 us (1%)
    pallas_call x1, Pallas kernels, on_device(): pl.pallas_call(kernel, out_shape=tuple((vmem(*s) for s in shapes + [((2 *...  47.3 us
    pallas_call x1, Pallas kernels, on_device(): pl.pallas_call(finish_kernel, out_shape=tuple((jax.ShapeDtypeStruct(*s) f...  2.77 us

profile of v11, /device:TPU:16, one launch (start us, length us, event | category | flops | bytes accessed | tf_op | source)
XLA Modules:
  0.0 50.7 jit_solution(18132371932425504559)
XLA Ops:
  0.6 47.3 %shard_map.102 = (f32[384,256]{1,0:T(8,128)S(1)}, bf16[6112,384]{1,0:T(8,128)(2,1)S(1)}, f32[32,1536]{1,0:T(8,128)S(1)}, bf16[16,12288]{1,0:T(8,128)(2,1)S(1)}, ...) custom-call(s32[4,128]{1,0:T(4,128)} %bitcast.4, bf16[512,1536]{1,0:T(8,128)(2,1)} %calib_hbm.1, ...), custom_call_target="tpu_custom_call" | custom-call | flops 2000000000 | bytes 16000000 | tf_op jit(solution)/shard_map/pallas_call | solution.py:497
  47.9 2.8 %shard_map.103 = (f32[384,256]{1,0:T(8,128)}, bf16[6112,384]{1,0:T(8,128)(2,1)}, f32[32,1536]{1,0:T(8,128)}, bf16[16,12288]{1,0:T(8,128)(2,1)}) custom-call(f32[384,256]{1,0:T(8,128)S(1)} %get-tuple-element.14.pruned, bf16[6112,384]{1,0:T(8,128)(2,1)S(1)} %get-tuple-element.15.rest, f32[32,1536]{1,0:T(8,128)S(1)} %get-tuple-element.16.hess, ...), custom_call_target="tpu_custom_call" | custom-call | flops 600000000 | bytes 12000000 | tf_op jit(solution)/shard_map/pallas_call | solution.py:554
